TPU v7x, 128 devices: a whole 4x4x4 slice. The times are simulated.
128 devices in a mesh: exp: 4 (over x), patch: 32 (over z, y, core).
Axes of the slice: x: 4, y: 4, z: 4, core: 2. Of those that a mesh axis runs over, the one named last changes fastest.
Arguments:
- images: bfloat16 [1024, 512, 512], P(('exp', 'patch')), may hold values from -6 to 6
- variance: bfloat16 [1024, 512, 512], P(('exp', 'patch')), may hold values from 0.5 to 8
- kernel_x: bfloat16 [16, 21], replicated, may hold values from -1.25 to 1.25
- kernel_y: bfloat16 [16, 21], replicated, may hold values from -1.25 to 1.25
- coef: float32 [1024, 16], P(('exp', 'patch')), may hold values from -1.5 to 1.5
- exposure_filter: int32 [1024], P(('exp', 'patch')), may hold values from 0 to 5
- block_patch: int32 [1024, 16], P(('exp', 'patch')), may hold values from 0 to 511, as said below
- patch_home: int32 [128], replicated, may hold values from 0 to 127, as said below
Outputs:
- coadd: float32 [128, 6, 256, 256], P('patch', None, 'exp')
Inputs may be any that keep to these rules, and one draw needn't show every extreme that they name: `block_patch`: entry 4 p + q names quadrant q of patch p. Of the 128 blocks of the cells of one device, at most 6 go to patches with the same patch_home // 4, and on every device exactly 6 go to one such value. `patch_home`: each number once.
All inputs are finite; a program needn't handle non-finite values.
Results may differ from a plain program's by a relative error of at most 0.0052.
Values may be sent and summed in bfloat16 or wider, within the bound.
A program may use at most 192 MiB of HBM per device.

v0:
```python
import functools

import jax
import jax.numpy as jnp
from jax import lax
from jax.experimental import pallas as pl
from jax.experimental.pallas import tpu as pltpu
from jax.sharding import PartitionSpec as P

FILTERS = 6
TAPS = 21
BASIS = 16
CHUNKS = 4
CAP = 4
EXTRA = 2
ALL = CAP + EXTRA
LOOSE = 2
NONE = 96
BF16 = jnp.bfloat16
F32 = jnp.float32


def trade_groups(vs):
    grp = lax.broadcasted_iota(jnp.int32, vs[0].shape, 1) // 16
    a = [v if i == 0 else pltpu.roll(v, 16 * i, 1) for i, v in enumerate(vs)]
    a = [a[-j % 8] for j in range(8)]
    for s in (1, 2, 4):
        pick = (grp & s) != 0
        a = [jnp.where(pick, a[(j - s) % 8], a[j]) for j in range(8)]
    return [v if j == 0 else pltpu.roll(v, 128 - 16 * j, 1) for j, v in enumerate(a)]


def trade_rows(a, b):
    upper = lax.broadcasted_iota(jnp.int32, a.shape, a.ndim - 2) < 4
    axis = a.ndim - 2
    return (
        jnp.where(upper, a, pltpu.roll(b, 4, axis)),
        jnp.where(upper, pltpu.roll(a, 4, axis), b),
    )


def block_tiles(tmp, b):
    halves = [
        trade_groups([tmp[b, pl.ds(8 * h + i, 8, stride=16), :] for i in range(8)])
        for h in range(2)
    ]
    return [jnp.concatenate([halves[0][j], halves[1][j]], axis=1) for j in range(8)]


def strip_tiles(ref, tmp, by):
    rows = pl.ds(pl.multiple_of(by * 128, 128), 128)
    for b in range(4):
        tmp[b] = ref[0, rows, pl.ds(128 * b, 128)].astype(F32)
    return [block_tiles(tmp, b) for b in range(4)]


def convolve(src, wts, acc, chunk, slot):
    lhs = [
        jnp.concatenate(
            [src[pl.ds(b * 8 + 2 * chunk + dx, 2)].reshape(64, 768) for b in range(4)], axis=0
        )
        for dx in range(3)
    ]
    total = jnp.dot(jnp.concatenate(lhs, axis=1), wts[...], preferred_element_type=F32)
    acc[slot] = total.reshape(4, 2, 32, 256)


def finish(var, tmp, acc, blocks, slot, chunks):
    def block_row(by, _):
        row0 = pl.multiple_of(by * 8, 8)
        for b, vs in enumerate(strip_tiles(var, tmp, by)):
            for i, c in enumerate(chunks):
                weight = 1.0 / jnp.concatenate(vs[2 * c : 2 * c + 2], axis=0)
                got = jnp.concatenate([acc[i, b, j, pl.ds(row0, 8), :] for j in range(2)], axis=0)
                blocks[slot, i, by * 4 + b, pl.ds(0, 16)] = (got * weight).astype(BF16)
                blocks[slot, i, by * 4 + b, pl.ds(16, 16)] = weight.astype(BF16)
        return 0

    lax.fori_loop(0, 4, block_row, 0)


def drain(blocks, outs, sems, slot):
    def one(i, _):
        pltpu.make_async_copy(blocks.at[slot, 0, 0], outs[0][0].at[0, pl.ds(0, 32)], sems.at[slot]).wait()
        return 0

    lax.fori_loop(0, 16 * len(outs), one, 0)


def scatter(dest, blocks, outs, sems, cell, cells, slot):
    def send(b, _):
        where = dest[cell * 16 + b]
        owner, rank = where // 8, lax.rem(where, 8)

        def copy(i, target):
            pltpu.make_async_copy(blocks.at[slot, i, b], target, sems.at[slot]).start()

        def rows(k):
            return pl.ds(pl.multiple_of(k * 32, 32), 32)

        if outs[0][1] is None:
            for i, (main, _) in enumerate(outs):
                copy(i, main.at[owner, rows(rank)])
            return 0

        @pl.when(rank < CAP)
        def _():
            for i, (main, _) in enumerate(outs):
                copy(i, main.at[owner, rows(rank)])

        @pl.when(rank >= CAP)
        def _():
            for i, (_, extra) in enumerate(outs):
                copy(i, extra.at[owner, rows(rank - CAP)])

        return 0

    lax.fori_loop(0, 16, send, 0)

    @pl.when(cell == cells - 1)
    def _():
        drain(blocks, outs, sems, slot)
        drain(blocks, outs, sems, 1 - slot)


def build_weights(coef, bx, ry, rolled, wts):
    scaled = (coef[0] * ry[...]).astype(BF16)
    core = jnp.dot(bx[...], scaled, preferred_element_type=F32)
    side = jnp.zeros((48, 256), F32)
    wide = jnp.concatenate([side, core, side], axis=1)
    for r in range(8):
        turned = wide if r == 0 else pltpu.roll(wide, 1024 - 16 * r, 1)
        rolled[r] = turned.astype(BF16)
    for jy in range(48):
        start = 47 - jy
        r, base = start % 8, start // 8 * 128
        for dx in range(3):
            wts[pl.ds(dx * 768 + jy * 16, 16), :] = rolled[
                r, pl.ds(dx * 16, 16), pl.ds(base, 256)
            ]


def clear_edges(tiles, src):
    tiles[:, 0:8, :] = jnp.zeros((32, 8, 256), F32)
    tiles[:, 40:48, :] = jnp.zeros((32, 8, 256), F32)
    src[0] = jnp.zeros((32, 768), BF16)
    src[33] = jnp.zeros((32, 768), BF16)


def stack_rows(tiles, src, t):
    for dy in range(3):
        src[1 + t, :, pl.ds(dy * 256, 256)] = tiles[t, pl.ds(7 + dy, 32), :].astype(BF16)


def first_kernel(
    dest, img, var, coef, bx, ry, codes, out, tiled, free, *scratch
):
    tiles, src, tmp, rolled, wts, acc, blocks, sems, code_sem, wide = scratch
    cell, cells = pl.program_id(0), pl.num_programs(0)
    slot = lax.rem(cell, 2)

    @pl.when(cell == 0)
    def _():
        clear_edges(tiles, src)

    build_weights(coef, bx, ry, rolled, wts)

    def tile_block(by, _):
        row0 = pl.multiple_of(8 + by * 8, 8)
        for b, vs in enumerate(strip_tiles(img, tmp, by)):
            for j, v in enumerate(vs):
                tiles[b * 8 + j, pl.ds(row0, 8), :] = v
        return 0

    lax.fori_loop(0, 4, tile_block, 0)

    def stack_some(b, _):
        for k in range(3):
            stack_rows(tiles, src, b * 8 + k)

        @pl.when(b > 0)
        def _():
            stack_rows(tiles, src, b * 8 - 1)

        return 0

    lax.fori_loop(0, 4, stack_some, 0)

    def keep(t, _):
        tiled[0, t] = tiles[t, pl.ds(8, 32), :].astype(BF16)
        return 0

    lax.fori_loop(0, 32, keep, 0, unroll=8)

    convolve(src, wts, acc, 0, 0)

    @pl.when(cell >= 2)
    def _():
        drain(blocks, [(out, None)], sems, slot)

    finish(var, tmp, acc, blocks, slot, [0])
    scatter(dest, blocks, [(out, None)], sems, cell, cells, slot)

    for k in range(LOOSE):
        which = dest[cells * 16 + k]

        @pl.when(which // 16 == cell)
        def _(k=k, which=which):
            by, b = lax.rem(which, 16) // 4, lax.rem(which, 4)
            for j in range(3, 8):
                stack_rows(tiles, src, b * 8 + j)
            lhs = [src[pl.ds(b * 8 + dx, 8)].reshape(256, 768) for dx in range(3)]
            total = jnp.dot(
                jnp.concatenate(lhs, axis=1), wts[...], preferred_element_type=F32
            )
            wide[...] = total.reshape(8, 32, 256)
            rows = pl.ds(pl.multiple_of(by * 128, 128), 128)
            cols = pl.ds(pl.multiple_of(b * 128, 128), 128)
            tmp[0] = var[0, rows, cols].astype(F32)
            vs = block_tiles(tmp, 0)
            row0 = pl.multiple_of(by * 8, 8)
            for c in range(1, CHUNKS):
                weight = 1.0 / jnp.concatenate(vs[2 * c : 2 * c + 2], axis=0)
                got = jnp.concatenate(
                    [wide[2 * c + j, pl.ds(row0, 8), :] for j in range(2)], axis=0
                )
                free[c - 1, k, pl.ds(0, 16)] = (got * weight).astype(BF16)
                free[c - 1, k, pl.ds(16, 16)] = weight.astype(BF16)

    @pl.when(cell == cells - 1)
    def _():
        copy = pltpu.make_async_copy(codes, out.at[:, pl.ds(ALL * 32, 16)], code_sem)
        copy.start()
        copy.wait()


def other_kernel(dest, tiled, var, coef, bx, ry, *rest):
    outs, rest = rest[: 2 * (CHUNKS - 1)], rest[2 * (CHUNKS - 1) :]
    outs = [outs[2 * i : 2 * i + 2] for i in range(CHUNKS - 1)]
    tiles, src, tmp, rolled, wts, acc, blocks, sems = rest
    cell, cells = pl.program_id(0), pl.num_programs(0)
    slot = lax.rem(cell, 2)

    @pl.when(cell == 0)
    def _():
        clear_edges(tiles, src)

    build_weights(coef, bx, ry, rolled, wts)

    def stack_all(t, _):
        tiles[t, pl.ds(8, 32), :] = tiled[0, t].astype(F32)
        stack_rows(tiles, src, t)
        return 0

    lax.fori_loop(0, 32, stack_all, 0, unroll=4)

    for i in range(CHUNKS - 1):
        convolve(src, wts, acc, i + 1, i)

    @pl.when(cell >= 2)
    def _():
        drain(blocks, outs, sems, slot)

    finish(var, tmp, acc, blocks, slot, list(range(1, CHUNKS)))
    scatter(dest, blocks, outs, sems, cell, cells, slot)


def match_cells(dest, images, variance, coef_rows, band_x, rows_y, codes):
    cells = images.shape[0]
    owners = codes.shape[0]
    out = [
        jax.ShapeDtypeStruct((owners, CAP * 32, 256), BF16),
        jax.ShapeDtypeStruct((owners, EXTRA * 32, 256), BF16),
    ]
    out_codes = jax.ShapeDtypeStruct((owners, ALL * 32 + 16, 256), BF16)
    pixels = pl.BlockSpec((1, 512, 512), lambda i, d: (i, 0, 0))
    tiled_spec = pl.BlockSpec((1, 32, 32, 256), lambda i, d: (i, 0, 0, 0))
    tables = [
        pl.BlockSpec((1, 256, 1), lambda i, d: (i, 0, 0)),
        pl.BlockSpec((48, 256), lambda i, d: (0, 0)),
        pl.BlockSpec((256, 512), lambda i, d: (0, 0)),
    ]
    params = pltpu.CompilerParams(vmem_limit_bytes=48 * 2**20)
    cost = pl.CostEstimate(flops=9000000000, bytes_accessed=30000000, transcendentals=0)

    def scratch(chunks):
        return [
            pltpu.VMEM((32, 48, 256), F32),
            pltpu.VMEM((34, 32, 768), BF16),
            pltpu.VMEM((4, 128, 128), F32),
            pltpu.VMEM((8, 48, 1024), BF16),
            pltpu.VMEM((2304, 256), BF16),
            pltpu.VMEM((chunks, 4, 2, 32, 256), F32),
            pltpu.VMEM((2, chunks, 16, 32, 256), BF16),
            pltpu.SemaphoreType.DMA((2,)),
        ]

    first, tiled, free = pl.pallas_call(
        first_kernel,
        out_shape=[
            out_codes,
            jax.ShapeDtypeStruct((cells, 32, 32, 256), BF16),
            jax.ShapeDtypeStruct((CHUNKS - 1, LOOSE, 32, 256), BF16),
        ],
        grid_spec=pltpu.PrefetchScalarGridSpec(
            num_scalar_prefetch=1,
            grid=(cells,),
            in_specs=[
                pixels,
                pixels,
                *tables,
                pl.BlockSpec((owners, 16, 256), lambda i, d: (0, 0, 0)),
            ],
            out_specs=[
                pl.BlockSpec(memory_space=pl.ANY),
                tiled_spec,
                pl.BlockSpec((CHUNKS - 1, LOOSE, 32, 256), lambda i, d: (0, 0, 0, 0)),
            ],
            scratch_shapes=[
                *scratch(1),
                pltpu.SemaphoreType.DMA,
                pltpu.VMEM((8, 32, 256), F32),
            ],
        ),
        compiler_params=params,
        cost_estimate=cost,
        name="match_first",
    )(dest, images, variance, coef_rows, band_x, rows_y, codes)
    others = pl.pallas_call(
        other_kernel,
        out_shape=out * (CHUNKS - 1),
        grid_spec=pltpu.PrefetchScalarGridSpec(
            num_scalar_prefetch=1,
            grid=(cells,),
            in_specs=[tiled_spec, pixels, *tables],
            out_specs=[pl.BlockSpec(memory_space=pl.ANY)] * (2 * (CHUNKS - 1)),
            scratch_shapes=scratch(CHUNKS - 1),
        ),
        compiler_params=params,
        cost_estimate=cost,
        name="match_others",
    )(dest, tiled, variance, coef_rows, band_x, rows_y)
    return free, [first, *others[0::2]], others[1::2]


def add_kernel(begin, code, group, got, *rest):
    free, outs, acc = rest[:-5], rest[-5:-1], rest[-1]
    step = pl.program_id(0)
    per = got.shape[0]

    @pl.when(step == 0)
    def _():
        acc[...] = jnp.zeros_like(acc)

    def one(i, _):
        at = (step * per + i) * 8
        for r in range(got.shape[1] // 32):
            acc[code[at + begin + r]] += got[i, pl.ds(32 * r, 32), :].astype(F32)
        for r in range(LOOSE if free else 0):
            plane = code[at + ALL + r]

            @pl.when(plane != NONE)
            def _(r=r, plane=plane):
                acc[plane] += free[0][i, pl.ds(32 * r, 32), :].astype(F32)

        return 0

    lax.fori_loop(0, per, one, 0)

    @pl.when(step == pl.num_programs(0) - 1)
    def _():
        def put(p, _):
            for s, out in enumerate(outs):
                share = lax.rem(group[0] + s, 4)
                both = acc[share // 2 * 48 + p]
                fields = both.reshape(2, 16, 256)
                halves = trade_rows(fields[:, :8], fields[:, 8:])
                part = jnp.where(lax.rem(share, 2) == 0, halves[0], halves[1])
                out[p] = part.reshape(16, 256).astype(BF16)
            return 0

        lax.fori_loop(0, 48, put, 0, unroll=2)
        for out in outs:
            out[48] = jnp.full((16, 256), group[1].astype(F32), F32).astype(BF16)


def add_slots(code, group, got, begin, free=None, part=0):
    steps = 2
    per = got.shape[0] // steps
    count = got.shape[1] // 32 * 32
    share = jax.ShapeDtypeStruct((49, 16, 256), BF16)
    specs = [pl.BlockSpec((per, count, 256), lambda i, d, g: (i, 0, 0))]
    if free is not None:
        specs.append(pl.BlockSpec((per, LOOSE * 32, 256), lambda i, d, g: (i, part, 0)))
    return pl.pallas_call(
        functools.partial(add_kernel, begin),
        out_shape=[share] * 4,
        grid_spec=pltpu.PrefetchScalarGridSpec(
            num_scalar_prefetch=2,
            grid=(steps,),
            in_specs=specs,
            out_specs=[pl.BlockSpec((49, 16, 256), lambda i, d, g: (0, 0, 0))] * 4,
            scratch_shapes=[pltpu.VMEM((NONE + 1, 32, 256), F32)],
        ),
        compiler_params=pltpu.CompilerParams(vmem_limit_bytes=48 * 2**20),
        cost_estimate=pl.CostEstimate(flops=6000000, bytes_accessed=6000000, transcendentals=0),
        name="add_slots",
    )(code, group, got, *([] if free is None else [free]))


def ratio_kernel(counts, *refs):
    ins, out, lines = refs[:-2], refs[-2], refs[-1]
    starts = [sum(counts[:c]) for c in range(CHUNKS)]

    def half(qx, _):
        def one(i, _):
            f = i * 2
            vs = []
            for c in range(CHUNKS):
                pair = []
                for k in range(2):
                    total = ins[starts[c]][qx * 6 + f + k].astype(F32)
                    for s in range(1, counts[c]):
                        total += ins[starts[c] + s][qx * 6 + f + k].astype(F32)
                    pair.append(total[:8] / jnp.maximum(total[8:], 1.0))
                vs.extend(trade_rows(*pair))
            for h in range(2):
                got = trade_groups([v[:, 128 * h : 128 * h + 128] for v in vs])
                for k, line in enumerate(got):
                    lines[pl.ds(f * 64 + 8 * h + k, 8, stride=16), :] = line
            return 0

        lax.fori_loop(0, 3, one, 0, unroll=3)
        out[0, :, pl.ds(pl.multiple_of(qx * 128, 128), 128)] = lines[...]
        return 0

    lax.fori_loop(0, 2, half, 0)


def ratio(shares):
    counts = [len(share) for share in shares]
    parts = [x for share in shares for x in share]
    patches = parts[0].shape[0] // 12
    out = pl.pallas_call(
        functools.partial(ratio_kernel, counts),
        grid=(patches,),
        out_shape=jax.ShapeDtypeStruct((patches, FILTERS * 64, 256), F32),
        in_specs=[pl.BlockSpec((12, 16, 256), lambda i: (i, 0, 0))] * len(parts),
        out_specs=pl.BlockSpec((1, FILTERS * 64, 256), lambda i: (i, 0, 0)),
        scratch_shapes=[pltpu.VMEM((FILTERS * 64, 128), F32)],
        compiler_params=pltpu.CompilerParams(vmem_limit_bytes=48 * 2**20),
        name="ratio",
    )(*parts)
    return out.reshape(patches, FILTERS, 64, 256)


def tap_tables(kernel_x, kernel_y):
    jx = jnp.arange(48)[:, None]
    ix = jnp.arange(16)[None, :]
    pick = ((jx - ix - 6)[None] == jnp.arange(TAPS)[:, None, None]).astype(BF16)
    band_x = jnp.einsum("kt,tji->jki", kernel_x, pick, preferred_element_type=F32)
    band_x = band_x.astype(BF16).reshape(48, BASIS * 16)
    line = jnp.arange(512)
    tap = jnp.arange(TAPS)
    pick_y = (41 - (line // 16 + 16)[None, :] == tap[:, None]).astype(BF16)
    taps_y = jnp.dot(kernel_y, pick_y, preferred_element_type=F32).astype(BF16)
    row = jnp.arange(BASIS * 16)
    spread = (row[:, None] // 16 == jnp.arange(BASIS)[None, :]).astype(BF16)
    rows_y = jnp.dot(spread, taps_y, preferred_element_type=F32)
    rows_y = jnp.where(row[:, None] % 16 == line[None, :] % 16, rows_y, 0.0)
    return band_x, rows_y


def exchange(planes, groups):
    moved = [planes[0]]
    for s in range(1, groups):
        ring = [(i, (i + s) % groups) for i in range(groups)]
        moved.append(lax.ppermute(planes[s], "exp", ring))
    return moved


def on_device(images, variance, kernel_x, kernel_y, coef, exposure_filter, block_patch, patch_home):
    cell_count = images.shape[0]
    owner_count = lax.axis_size("patch")
    patches_local = patch_home.shape[0] // owner_count
    block_count = cell_count * 16

    targets = block_patch.reshape(-1)
    patch_index = targets // 4
    quadrant = targets % 4
    home_slot = jnp.sum(
        jnp.where(
            patch_index[:, None] == jnp.arange(patch_home.shape[0])[None, :], patch_home[None, :], 0
        ),
        axis=1,
    )
    owner_index = home_slot // patches_local
    local_patch = home_slot % patches_local
    band_index = jnp.repeat(exposure_filter, 16)
    order = jnp.arange(block_count)
    earlier = order[None, :] < order[:, None]
    rank = jnp.sum((owner_index[:, None] == owner_index[None, :]) & earlier, axis=1)
    late = rank >= CAP
    late_rank = jnp.sum(late[None, :] & earlier, axis=1)
    loose = late & (late_rank < LOOSE)
    more = jnp.any(late & (late_rank >= LOOSE))
    which = loose & (late_rank == jnp.arange(LOOSE)[:, None])
    which = jnp.max(jnp.where(which, order, -16), axis=1)
    dest = jnp.concatenate([owner_index * 8 + rank, which]).astype(jnp.int32)
    code = (
        (quadrant // 2) * 48 + (local_patch * 2 + quadrant % 2) * FILTERS + band_index
    )
    place = jnp.where(loose, ALL + late_rank, -1)
    more_place = jnp.where(late & ~loose, rank, -1)
    owners = jnp.arange(owner_count)[:, None, None]
    row = jnp.arange(16)[:, None]
    here = (rank == row) | (place == row) | (more_place + 5 == row) & (row >= 9)
    codes = jnp.min(jnp.where((owner_index == owners) & here, code, NONE), axis=2)
    codes = jnp.where(jnp.arange(16) == 8, more.astype(code.dtype), codes)
    codes = jnp.pad(codes.astype(BF16)[:, None, :], ((0, 0), (0, 15), (0, 240)))

    band_x, rows_y = tap_tables(kernel_x, kernel_y)
    coef_rows = jnp.repeat(coef, 16, axis=1)[:, :, None]
    free, mains, extras = match_cells(dest, images, variance, coef_rows, band_x, rows_y, codes)

    groups = lax.axis_size("exp")
    def send(part):
        return lax.all_to_all(part, "patch", 0, 0, tiled=True)

    gathered = lax.all_gather(free.reshape(-1, 256), "patch")
    got_0 = send(mains[0])
    head = got_0[:, ALL * 32, :16].astype(jnp.int32)
    got_code = head[:, :8].reshape(-1)
    group = jnp.stack([lax.axis_index("exp"), jnp.max(head[:, 8])])

    def add(got, c):
        return add_slots(got_code, group, got, 0, gathered, c - 1)

    hold = lax.optimization_barrier
    planes_0 = add_slots(got_code, group, got_0, 0)
    share_0 = exchange(planes_0, groups)
    got_1 = send(mains[1])
    part_2, own = hold((mains[2], planes_0[0]))
    share_0[0] = own
    planes_1 = add(got_1, 1)
    share_1 = exchange(planes_1, groups)
    got_2 = send(part_2)
    part_3, share_0, share_1[0] = hold((mains[3], share_0, share_1[0]))
    share_2 = exchange(add(got_2, 2), groups)
    got_3, share_1 = hold((send(part_3), share_1))
    share_3 = exchange(add(got_3, 3), groups)
    shares = [share_0, share_1, share_2, share_3]

    def plain(shares, extras, head):
        return ratio(shares)

    def with_more(shares, extras, head):
        codes = jnp.concatenate([head[:, :CAP], head[:, 9 : 9 + EXTRA], head[:, :2]], axis=1)
        parts = [shares[0]]
        for share, extra in zip(shares[1:], extras, strict=True):
            planes = add_slots(codes.reshape(-1), group, send(extra), CAP)
            parts.append([*share, *exchange(planes, groups)])
        return ratio(parts)

    more = functools.reduce(jnp.maximum, [x[48, 0, 0] for x in share_0]) > 0
    return lax.cond(more, with_more, plain, shares, extras, head)


def solution(mesh):
    return jax.shard_map(
        on_device,
        mesh=mesh,
        in_specs=(
            P(("exp", "patch"), None, None),
            P(("exp", "patch"), None, None),
            P(),
            P(),
            P(("exp", "patch"), None),
            P(("exp", "patch")),
            P(("exp", "patch"), None),
            P(),
        ),
        out_specs=P("patch", None, "exp", None),
        check_vma=False,
    )
```

profile of v0, /device:TPU:1, one launch (start us, length us, event | category | flops | bytes accessed | tf_op | source)
XLA Modules:
  0.0 251.7 jit_solution(18015436668800184893)
XLA Ops:
  14.3 34.1 %match_first.1 = (bf16[32,208,256]{2,1,0:T(8,128)(2,1)S(1)}, bf16[8,32,32,256]{3,2,1,0:T(8,128)(2,1)}, bf16[3,2,32,256]{3,2,1,0:T(8,128)(2,1)}) custom-call(s32[130]{0:T(256)S(1)} %pad_add_fusion.1.dest, bf16[8,512,512]{2,1,0:T(8,128)(2,1)} %img.1, bf16[8,512,512]{2,1,0:T(8,128)(2,1)} %var.3, f32[8,256,1]{2,1,0:T(8,128)S(1)} %broadcast_in_dim_reshape.4.coef, ...), custom_call_target="tpu_custom_call" | custom-call | flops 8999999488 | bytes 30000000 | tf_op jit(solution)/shard_map/match_first/pallas_call | solution.py:298
  48.4 1.7 copy-done.1
  50.1 9.6 %all-to-all-start.3 = ((bf16[32,208,256]{2,1,0:T(8,128)(2,1)}), bf16[32,208,256]{2,1,0:T(8,128)(2,1)S(1)}, u32[]{:S(2)}, u32[]{:S(2)}) async-start(bf16[32,208,256]{2,1,0:T(8,128)(2,1)} %copy-done.1), calls=%async_computation.3 | async-start | bytes 6815744 | tf_op jit(solution)/shard_map/all_to_all | solution.py:528
  62.7 36.4 %match_others.1 = (bf16[32,128,256]{2,1,0:T(8,128)(2,1)S(1)}, bf16[32,64,256]{2,1,0:T(8,128)(2,1)}, bf16[32,128,256]{2,1,0:T(8,128)(2,1)S(1)}, bf16[32,64,256]{2...) custom-call(s32[130]{0:T(256)S(1)} %pad_add_fusion.1.dest, ...), custom_call_target="tpu_custom_call" | custom-call | flops 8999999488 | bytes 30000000 | tf_op jit(solution)/shard_map/match_others/pallas_call | solution.py:329
  102.8 7.6 %all-to-all-start.4 = ((bf16[32,128,256]{2,1,0:T(8,128)(2,1)}), bf16[32,128,256]{2,1,0:T(8,128)(2,1)}, u32[]{:S(2)}, u32[]{:S(2)}) async-start(bf16[32,128,256]{2,1,0:T(8,128)(2,1)} %copy-done.3), calls=%async_computation.4 | async-start | bytes 4194304 | tf_op jit(solution)/shard_map/all_to_all | solution.py:528
  112.1 4.1 %add_slots.10 = (bf16[49,16,256]{2,1,0:T(8,128)(2,1)}, bf16[49,16,256]{2,1,0:T(8,128)(2,1)S(1)}, bf16[49,16,256]{2,1,0:T(8,128)(2,1)}, bf16[49,16,256]{2,1,0:T(8,128)(2,1)S(1)}) custom-call(s32[256]{0:T(256)S(1)} %reshape.362.code, s32[2]{0:T(128)S(1)} %pad_add_fusion.2.group, bf16[32,208,256]{2,1,0:T(8,128)(2,1)S(1)} %all-to-all-done.3.got), custom_call_target="tpu_custom_call" | custom-call | flops 6000000 | bytes 6000000 | tf_op jit(solution)/shard_map/add_slots/pallas_call | solution.py:395
  117.7 26.6 %all-to-all-done.4.got = bf16[32,128,256]{2,1,0:T(8,128)(2,1)} async-done(((bf16[32,128,256]{2,1,0:T(8,128)(2,1)}), bf16[32,128,256]{2,1,0:T(8,128)(2,1)}, u32[]{:S(2)}, u32[]{:S(2)}) %all-to-all-start.4) | async-done | bytes 2097184 | tf_op jit(solution)/shard_map/all_to_all | solution.py:528
  144.3 4.6 %all-to-all-start.6 = ((bf16[32,128,256]{2,1,0:T(8,128)(2,1)}), bf16[32,128,256]{2,1,0:T(8,128)(2,1)S(1)}, u32[]{:S(2)}, u32[]{:S(2)}) async-start(bf16[32,128,256]{2,1,0:T(8,128)(2,1)} %copy-done.2), calls=%async_computation.6 | async-start | bytes 4194304 | tf_op jit(solution)/shard_map/all_to_all | solution.py:528
  149.0 2.8 %collective-permute-start.10 = (bf16[49,16,256]{2,1,0:T(8,128)(2,1)}, bf16[49,16,256]{2,1,0:T(8,128)(2,1)}, u32[]{:S(2)}, u32[]{:S(2)}) collective-permute-start(bf16[49,16,256]{2,1,0:T(8,128)(2,1)} %get-tuple-element.176), channel_id=1, source_target_pairs={{0,64},{32,96},{64,0},{96,32},{1,65},{33,97},{65,1},{97,33},{2,66}... | collective-permute-start | bytes 1204232 | tf_op jit(solution)/shard_map/ppermute | solution.py:478
  153.2 5.6 %add_slots.11 = (bf16[49,16,256]{2,1,0:T(8,128)(2,1)}, bf16[49,16,256]{2,1,0:T(8,128)(2,1)}, bf16[49,16,256]{2,1,0:T(8,128)(2,1)}, bf16[49,16,256]{2,1,0:T(8,128)(2,1)S(1)}) custom-call(s32[256]{0:T(256)S(1)} %reshape.362.code, s32[2]{0:T(128)S(1)} %pad_add_fusion.2.group, bf16[32,128,256]{2,1,0:T(8,128)(2,1)} %all-to-all-done.4.got, ...), custom_call_target="tpu_custom_call" | custom-call | flops 6000000 | bytes 6000000 | tf_op jit(solution)/shard_map/add_slots/pallas_call | solution.py:395
  158.8 2.7 %collective-permute-done.10 = bf16[49,16,256]{2,1,0:T(8,128)(2,1)} collective-permute-done((bf16[49,16,256]{2,1,0:T(8,128)(2,1)}, bf16[49,16,256]{2,1,0:T(8,128)(2,1)}, u32[]{:S(2)}, u32[]{:S(2)}) %collective-permute-start.10) | collective-permute-done | bytes 401440 | tf_op jit(solution)/shard_map/ppermute | solution.py:478
  161.5 8.6 %collective-permute-done.11 = bf16[49,16,256]{2,1,0:T(8,128)(2,1)} collective-permute-done((bf16[49,16,256]{2,1,0:T(8,128)(2,1)S(1)}, bf16[49,16,256]{2,1,0:T(8,128)(2,1)}, u32[]{:S(2)}, u32[]{:S(2)}) %collective-permute-start.11) | collective-permute-done | bytes 401440 | tf_op jit(solution)/shard_map/ppermute | solution.py:478
  170.7 6.2 %all-to-all-done.6.got = bf16[32,128,256]{2,1,0:T(8,128)(2,1)S(1)} async-done(((bf16[32,128,256]{2,1,0:T(8,128)(2,1)}), bf16[32,128,256]{2,1,0:T(8,128)(2,1)S(1)}, u32[]{:S(2)}, u32[]{:S(2)}) %all-to-all-start.6) | async-done | bytes 2097184 | tf_op jit(solution)/shard_map/all_to_all | solution.py:528
  177.0 6.7 %all-to-all-start.5 = ((bf16[32,128,256]{2,1,0:T(8,128)(2,1)}), bf16[32,128,256]{2,1,0:T(8,128)(2,1)}, u32[]{:S(2)}, u32[]{:S(2)}) async-start(bf16[32,128,256]{2,1,0:T(8,128)(2,1)} %get-tuple-element.185), calls=%async_computation.5 | async-start | bytes 4194304 | tf_op jit(solution)/shard_map/all_to_all | solution.py:528
  184.9 2.4 collective-permute-start.13
  188.5 5.1 %add_slots.12 = (bf16[49,16,256]{2,1,0:T(8,128)(2,1)}, bf16[49,16,256]{2,1,0:T(8,128)(2,1)}, bf16[49,16,256]{2,1,0:T(8,128)(2,1)S(1)}, bf16[49,16,256]{2,1,0:T(8,128)(2,1)S(1)}) custom-call(s32[256]{0:T(256)S(1)} %reshape.362.code, s32[2]{0:T(128)S(1)} %pad_add_fusion.2.group, bf16[32,128,256]{2,1,0:T(8,128)(2,1)S(1)} %all-to-all-done.6.got, ...), custom_call_target="tpu_custom_call" | custom-call | flops 6000000 | bytes 6000000 | tf_op jit(solution)/shard_map/add_slots/pallas_call | solution.py:395
  197.2 8.1 %collective-permute-done.13 = bf16[49,16,256]{2,1,0:T(8,128)(2,1)S(1)} collective-permute-done((bf16[49,16,256]{2,1,0:T(8,128)(2,1)}, bf16[49,16,256]{2,1,0:T(8,128)(2,1)S(1)}, u32[]{:S(2)}, u32[]{:S(2)}) %collective-permute-start.13) | collective-permute-done | bytes 401440 | tf_op jit(solution)/shard_map/ppermute | solution.py:478
  206.1 5.6 %all-to-all-done.5.got = bf16[32,128,256]{2,1,0:T(8,128)(2,1)} async-done(((bf16[32,128,256]{2,1,0:T(8,128)(2,1)}), bf16[32,128,256]{2,1,0:T(8,128)(2,1)}, u32[]{:S(2)}, u32[]{:S(2)}) %all-to-all-start.5) | async-done | bytes 2097184 | tf_op jit(solution)/shard_map/all_to_all | solution.py:528
  211.7 4.6 %add_slots.13 = (bf16[49,16,256]{2,1,0:T(8,128)(2,1)S(1)}, bf16[49,16,256]{2,1,0:T(8,128)(2,1)S(1)}, bf16[49,16,256]{2,1,0:T(8,128)(2,1)S(1)}, bf16[49,16,256]{2,1,0:T(8,128)(2,1)S(1)}) custom-call(s32[256]{0:T(256)S(1)} %reshape.362.code, s32[2]{0:T(128)S(1)} %pad_add_fusion.2.group, bf16[32,128,256]{2,1,0:T(8,128)(2,1)} %all-to-all-done.5.got, ...), custom_call_target="tpu_custom_call" | custom-call | flops 6000000 | bytes 6000000 | tf_op jit(solution)/shard_map/add_slots/pallas_call | solution.py:395
  217.5 2.4 collective-permute-start.19
  227.7 4.1 %collective-permute-done.18 = bf16[49,16,256]{2,1,0:T(8,128)(2,1)S(1)} collective-permute-done((bf16[49,16,256]{2,1,0:T(8,128)(2,1)S(1)}, bf16[49,16,256]{2,1,0:T(8,128)(2,1)S(1)}, u32[]{:S(2)}, u32[]{:S(2)}) %collective-permute-start.18) | collective-permute-done | bytes 401440 | tf_op jit(solution)/shard_map/ppermute | solution.py:478
  231.8 7.9 %collective-permute-done.19 = bf16[49,16,256]{2,1,0:T(8,128)(2,1)S(1)} collective-permute-done((bf16[49,16,256]{2,1,0:T(8,128)(2,1)S(1)}, bf16[49,16,256]{2,1,0:T(8,128)(2,1)S(1)}, u32[]{:S(2)}, u32[]{:S(2)}) %collective-permute-start.19) | collective-permute-done | bytes 401440 | tf_op jit(solution)/shard_map/ppermute | solution.py:478
  239.7 5.1 %conditional.1 = (f32[4,6,64,256]{3,2,1,0:T(8,128)}) conditional(s32[]{:T(128)} %bitcast.10, (bf16[49,16,256]{2,1,0:T(8,128)(2,1)S(1)}, bf16[49,16,256]{2,1,0:T(8,128)(2,1)}, bf16[49,16,256]{2,1,0:T(8,128)(2,1)}, bf16[49,16,256]{2,1,0:T(8,128)(2,1)}, bf16[49,16,256]{2,1,0:T(8,128)(2,1)S(1)}, /*index=5*/bf16[49,16,256]{2,1,0:T(8,128)(2,1)S(1)}, ...), branch_computations={%region_7.8_spmd, %region_8.9_spmd} | conditional | flops 18000512 | bytes 59071388 | solution.py:566
  239.7 5.1 %ratio.2 = f32[4,384,256]{2,1,0:T(8,128)} custom-call(bf16[49,16,256]{2,1,0:T(8,128)(2,1)S(1)} %get-tuple-element.82.refs_0_, bf16[49,16,256]{2,1,0:T(8,128)(2,1)} %get-tuple-element.83.refs_1_, bf16[49,16,256]{2,1,0:T(8,128)(2,1)} %get-tuple-element.84.refs_2_, bf16[49,16,256]{2,1,0:T(8,128)(2,1)} %get-tuple-element.85.refs_3_, ...), custom_call_target="tpu_custom_call" | custom-call | tf_op jit(solution)/shard_map/cond/branch_0_fun/ratio/pallas_call | solution.py:444
  (98 shorter events, 32.2 us)
Async XLA Ops:
  12.1 36.3 %copy-start.4 = (f32[8,256,1]{2,1,0:T(8,128)}, f32[8,256,1]{2,1,0:T(8,128)S(1)}, u32[]{:S(2)}) copy-start(f32[8,256,1]{2,1,0:T(8,128)S(1)} %broadcast_in_dim_reshape.4.coef) | copy-start | bytes 24580
  14.3 34.1 %copy-start.6 = (f32[256,512]{1,0:T(8,128)}, f32[256,512]{1,0:T(8,128)S(1)}, u32[]{:S(2)}) copy-start(f32[256,512]{1,0:T(8,128)S(1)} %convolution_select_fusion.ry) | copy-start | bytes 1572868
  50.1 52.7 %all-to-all-start.3 = ((bf16[32,208,256]{2,1,0:T(8,128)(2,1)}), bf16[32,208,256]{2,1,0:T(8,128)(2,1)S(1)}, u32[]{:S(2)}, u32[]{:S(2)}) async-start(bf16[32,208,256]{2,1,0:T(8,128)(2,1)} %copy-done.1), calls=%async_computation.3 | async-start | bytes 6815744 | tf_op jit(solution)/shard_map/all_to_all | solution.py:528
  59.7 93.5 %all-gather.2.cloned.1.call-start = ((), (), s32[]{:S(2)}) async-start(), calls=%async_computation.7 | async-start | bytes 3244032 | tf_op jit(solution)/shard_map/all_gather | solution.py:530
  102.8 41.5 %all-to-all-start.4 = ((bf16[32,128,256]{2,1,0:T(8,128)(2,1)}), bf16[32,128,256]{2,1,0:T(8,128)(2,1)}, u32[]{:S(2)}, u32[]{:S(2)}) async-start(bf16[32,128,256]{2,1,0:T(8,128)(2,1)} %copy-done.3), calls=%async_computation.4 | async-start | bytes 4194304 | tf_op jit(solution)/shard_map/all_to_all | solution.py:528
  117.7 34.1 %copy-start.14 = (bf16[49,16,256]{2,1,0:T(8,128)(2,1)S(1)}, bf16[49,16,256]{2,1,0:T(8,128)(2,1)}, u32[]{:S(2)}) copy-start(bf16[49,16,256]{2,1,0:T(8,128)(2,1)} %copy-done.13) | copy-start | bytes 1204228
  117.7 34.9 %copy-start.12 = (bf16[49,16,256]{2,1,0:T(8,128)(2,1)S(1)}, bf16[49,16,256]{2,1,0:T(8,128)(2,1)}, u32[]{:S(2)}) copy-start(bf16[49,16,256]{2,1,0:T(8,128)(2,1)} %copy-done.11) | copy-start | bytes 1204228
  144.3 32.6 %all-to-all-start.6 = ((bf16[32,128,256]{2,1,0:T(8,128)(2,1)}), bf16[32,128,256]{2,1,0:T(8,128)(2,1)S(1)}, u32[]{:S(2)}, u32[]{:S(2)}) async-start(bf16[32,128,256]{2,1,0:T(8,128)(2,1)} %copy-done.2), calls=%async_computation.6 | async-start | bytes 4194304 | tf_op jit(solution)/shard_map/all_to_all | solution.py:528
  149.0 12.5 %collective-permute-start.10 = (bf16[49,16,256]{2,1,0:T(8,128)(2,1)}, bf16[49,16,256]{2,1,0:T(8,128)(2,1)}, u32[]{:S(2)}, u32[]{:S(2)}) collective-permute-start(bf16[49,16,256]{2,1,0:T(8,128)(2,1)} %get-tuple-element.176), channel_id=1, source_target_pairs={{0,64},{32,96},{64,0},{96,32},{1,65},{33,97},{65,1},{97,33},{2,66}... | collective-permute-start | bytes 1204232 | tf_op jit(solution)/shard_map/ppermute | solution.py:478
  151.8 18.3 %collective-permute-start.11 = (bf16[49,16,256]{2,1,0:T(8,128)(2,1)S(1)}, bf16[49,16,256]{2,1,0:T(8,128)(2,1)}, u32[]{:S(2)}, u32[]{:S(2)}) collective-permute-start(bf16[49,16,256]{2,1,0:T(8,128)(2,1)S(1)} %copy-done.14), channel_id=1, source_target_pairs={{0,96},{32,0},{64,32},{96,64},{1,97},{33,1},{65,33},{97,65},{2,98}... | collective-permute-start | bytes 1204232 | tf_op jit(solution)/shard_map/ppermute | solution.py:478
  152.7 18.1 %collective-permute-start.9 = (bf16[49,16,256]{2,1,0:T(8,128)(2,1)S(1)}, bf16[49,16,256]{2,1,0:T(8,128)(2,1)}, u32[]{:S(2)}, u32[]{:S(2)}) collective-permute-start(bf16[49,16,256]{2,1,0:T(8,128)(2,1)S(1)} %copy-done.12), channel_id=1, source_target_pairs={{0,32},{32,64},{64,96},{96,0},{1,33},{33,65},{65,97},{97,1},{2,34}... | collective-permute-start | bytes 1204232 | tf_op jit(solution)/shard_map/ppermute | solution.py:478
  177.0 34.7 %all-to-all-start.5 = ((bf16[32,128,256]{2,1,0:T(8,128)(2,1)}), bf16[32,128,256]{2,1,0:T(8,128)(2,1)}, u32[]{:S(2)}, u32[]{:S(2)}) async-start(bf16[32,128,256]{2,1,0:T(8,128)(2,1)} %get-tuple-element.185), calls=%async_computation.5 | async-start | bytes 4194304 | tf_op jit(solution)/shard_map/all_to_all | solution.py:528
  183.7 12.0 %collective-permute-start.12 = (bf16[49,16,256]{2,1,0:T(8,128)(2,1)}, bf16[49,16,256]{2,1,0:T(8,128)(2,1)S(1)}, u32[]{:S(2)}, u32[]{:S(2)}) collective-permute-start(bf16[49,16,256]{2,1,0:T(8,128)(2,1)} %get-tuple-element.187), channel_id=1, source_target_pairs={{0,32},{32,64},{64,96},{96,0},{1,33},{33,65},{65,97},{97,1},{2,34}... | collective-permute-start | bytes 1204232 | tf_op jit(solution)/shard_map/ppermute | solution.py:478
  184.9 20.3 %collective-permute-start.13 = (bf16[49,16,256]{2,1,0:T(8,128)(2,1)}, bf16[49,16,256]{2,1,0:T(8,128)(2,1)S(1)}, u32[]{:S(2)}, u32[]{:S(2)}) collective-permute-start(bf16[49,16,256]{2,1,0:T(8,128)(2,1)} %get-tuple-element.188), channel_id=1, source_target_pairs={{0,64},{32,96},{64,0},{96,32},{1,65},{33,97},{65,1},{97,33},{2,66}... | collective-permute-start | bytes 1204232 | tf_op jit(solution)/shard_map/ppermute | solution.py:478
  187.3 18.7 %collective-permute-start.14 = (bf16[49,16,256]{2,1,0:T(8,128)(2,1)S(1)}, bf16[49,16,256]{2,1,0:T(8,128)(2,1)}, u32[]{:S(2)}, u32[]{:S(2)}) collective-permute-start(bf16[49,16,256]{2,1,0:T(8,128)(2,1)S(1)} %get-tuple-element.189), channel_id=1, source_target_pairs={{0,96},{32,0},{64,32},{96,64},{1,97},{33,1},{65,33},{97,65},{2,98}... | collective-permute-start | bytes 1204232 | tf_op jit(solution)/shard_map/ppermute | solution.py:478
  193.6 26.3 %collective-permute-start.15 = (bf16[49,16,256]{2,1,0:T(8,128)(2,1)}, bf16[49,16,256]{2,1,0:T(8,128)(2,1)}, u32[]{:S(2)}, u32[]{:S(2)}) collective-permute-start(bf16[49,16,256]{2,1,0:T(8,128)(2,1)} %get-tuple-element.196), channel_id=1, source_target_pairs={{0,32},{32,64},{64,96},{96,0},{1,33},{33,65},{65,97},{97,1},{2,34}... | collective-permute-start | bytes 1204232 | tf_op jit(solution)/shard_map/ppermute | solution.py:478
  193.9 33.8 %collective-permute-start.16 = (bf16[49,16,256]{2,1,0:T(8,128)(2,1)S(1)}, bf16[49,16,256]{2,1,0:T(8,128)(2,1)}, u32[]{:S(2)}, u32[]{:S(2)}) collective-permute-start(bf16[49,16,256]{2,1,0:T(8,128)(2,1)S(1)} %get-tuple-element.197), channel_id=1, source_target_pairs={{0,64},{32,96},{64,0},{96,32},{1,65},{33,97},{65,1},{97,33},{2,66}... | collective-permute-start | bytes 1204232 | tf_op jit(solution)/shard_map/ppermute | solution.py:478
  195.7 43.9 %copy-start.17 = (bf16[49,16,256]{2,1,0:T(8,128)(2,1)S(1)}, bf16[49,16,256]{2,1,0:T(8,128)(2,1)}, u32[]{:S(2)}) copy-start(bf16[49,16,256]{2,1,0:T(8,128)(2,1)} %get-tuple-element.190) | copy-start | bytes 1204228
  195.7 43.9 %copy-start.25 = (bf16[49,16,256]{2,1,0:T(8,128)(2,1)S(1)}, bf16[49,16,256]{2,1,0:T(8,128)(2,1)}, u32[]{:S(2)}) copy-start(bf16[49,16,256]{2,1,0:T(8,128)(2,1)} %get-tuple-element.195) | copy-start | bytes 1204228
  195.7 32.0 %collective-permute-start.17 = (bf16[49,16,256]{2,1,0:T(8,128)(2,1)S(1)}, bf16[49,16,256]{2,1,0:T(8,128)(2,1)}, u32[]{:S(2)}, u32[]{:S(2)}) collective-permute-start(bf16[49,16,256]{2,1,0:T(8,128)(2,1)S(1)} %get-tuple-element.198), channel_id=1, source_target_pairs={{0,96},{32,0},{64,32},{96,64},{1,97},{33,1},{65,33},{97,65},{2,98}... | collective-permute-start | bytes 1204232 | tf_op jit(solution)/shard_map/ppermute | solution.py:478
  206.1 33.6 %copy-start.23 = (bf16[49,16,256]{2,1,0:T(8,128)(2,1)S(1)}, bf16[49,16,256]{2,1,0:T(8,128)(2,1)}, u32[]{:S(2)}) copy-start(bf16[49,16,256]{2,1,0:T(8,128)(2,1)} %copy-done.22) | copy-start | bytes 1204228
  216.3 15.5 %collective-permute-start.18 = (bf16[49,16,256]{2,1,0:T(8,128)(2,1)S(1)}, bf16[49,16,256]{2,1,0:T(8,128)(2,1)S(1)}, u32[]{:S(2)}, u32[]{:S(2)}) collective-permute-start(bf16[49,16,256]{2,1,0:T(8,128)(2,1)S(1)} %get-tuple-element.201), channel_id=1, source_target_pairs={{0,32},{32,64},{64,96},{96,0},{1,33},{33,65},{65,97},{97,1},{2,34}... | collective-permute-start | bytes 1204232 | tf_op jit(solution)/shard_map/ppermute | solution.py:478
  217.5 22.1 %collective-permute-start.19 = (bf16[49,16,256]{2,1,0:T(8,128)(2,1)S(1)}, bf16[49,16,256]{2,1,0:T(8,128)(2,1)S(1)}, u32[]{:S(2)}, u32[]{:S(2)}) collective-permute-start(bf16[49,16,256]{2,1,0:T(8,128)(2,1)S(1)} %get-tuple-element.202), channel_id=1, source_target_pairs={{0,64},{32,96},{64,0},{96,32},{1,65},{33,97},{65,1},{97,33},{2,66}... | collective-permute-start | bytes 1204232 | tf_op jit(solution)/shard_map/ppermute | solution.py:478
  219.9 19.7 %collective-permute-start.20 = (bf16[49,16,256]{2,1,0:T(8,128)(2,1)S(1)}, bf16[49,16,256]{2,1,0:T(8,128)(2,1)S(1)}, u32[]{:S(2)}, u32[]{:S(2)}) collective-permute-start(bf16[49,16,256]{2,1,0:T(8,128)(2,1)S(1)} %get-tuple-element.203), channel_id=1, source_target_pairs={{0,96},{32,0},{64,32},{96,64},{1,97},{33,1},{65,33},{97,65},{2,98}... | collective-permute-start | bytes 1204232 | tf_op jit(solution)/shard_map/ppermute | solution.py:478
  (14 other events, 132.8 us)
Sparse Core Ops, SparseCore 0:
  62.8 76.2 all-gather.1
where the time goes:
time: 253 us; the launch traced here: 252 us
  Pallas kernels  94.9 us (38%)
  waiting for transfers between devices  73 us (29%)
  starting transfers between devices  45.2 us (18%)
  between operations  16.9 us (7%)
  local copies, waits for them, and re-layouts  16.2 us (6%)
  other arithmetic  4.24 us (2%)
    all_to_all x4, waiting for transfers between devices, send(): return lax.all_to_all(part, 'patch', 0, 0, tiled=True)  39.4 us
    pallas_call x1, Pallas kernels, match_cells(): pl.pallas_call(other_kernel, out_shape=out * (CHUNKS - 1), grid_spec=pltp...  36.4 us
    pallas_call x1, Pallas kernels, match_cells(): pl.pallas_call(first_kernel, out_shape=[out_codes, jax.ShapeDtypeStruct((...  34.1 us
    ppermute x12, waiting for transfers between devices, exchange(): moved.append(lax.ppermute(planes[s], 'exp', ring))  32.9 us
    all_to_all x4, starting transfers between devices, send(): return lax.all_to_all(part, 'patch', 0, 0, tiled=True)  28.6 us
    pallas_call x4, Pallas kernels, add_slots(): pl.pallas_call(functools.partial(add_kernel, begin), out_shape=[share] *...  19.3 us
    ppermute x12, starting transfers between devices, exchange(): moved.append(lax.ppermute(planes[s], 'exp', ring))  16.5 us
    unnamed x42, local copies, waits for them, and re-layouts  9 us
  transfers between devices with their start and end apart: 17, of which 11 were waited for; matrix products, arithmetic and copies ran while one was open for 2% of the time, Pallas kernels for 22%

commit v1 on v0

--- a/solution.py
+++ b/solution.py
@@ -76,7 +76,7 @@
                 blocks[slot, i, by * 4 + b, pl.ds(16, 16)] = weight.astype(BF16)
         return 0
 
-    lax.fori_loop(0, 4, block_row, 0)
+    lax.fori_loop(0, 4, block_row, 0, unroll=2 if len(chunks) == 1 else 1)
 
 
 def drain(blocks, outs, sems, slot):
@@ -84,7 +84,7 @@
         pltpu.make_async_copy(blocks.at[slot, 0, 0], outs[0][0].at[0, pl.ds(0, 32)], sems.at[slot]).wait()
         return 0
 
-    lax.fori_loop(0, 16 * len(outs), one, 0)
+    lax.fori_loop(0, 16 * len(outs), one, 0, unroll=16)
 
 
 def scatter(dest, blocks, outs, sems, cell, cells, slot):
@@ -115,7 +115,7 @@
 
         return 0
 
-    lax.fori_loop(0, 16, send, 0)
+    lax.fori_loop(0, 16, send, 0, unroll=16)
 
     @pl.when(cell == cells - 1)
     def _():
@@ -184,13 +184,13 @@
 
         return 0
 
-    lax.fori_loop(0, 4, stack_some, 0)
+    lax.fori_loop(0, 4, stack_some, 0, unroll=4)
 
     def keep(t, _):
         tiled[0, t] = tiles[t, pl.ds(8, 32), :].astype(BF16)
         return 0
 
-    lax.fori_loop(0, 32, keep, 0, unroll=8)
+    lax.fori_loop(0, 32, keep, 0, unroll=32)
 
     convolve(src, wts, acc, 0, 0)
 
@@ -252,7 +252,7 @@
         stack_rows(tiles, src, t)
         return 0
 
-    lax.fori_loop(0, 32, stack_all, 0, unroll=4)
+    lax.fori_loop(0, 32, stack_all, 0, unroll=8)
 
     for i in range(CHUNKS - 1):
         convolve(src, wts, acc, i + 1, i)

time: 253 us -> 248 us (0.980)
  Pallas kernels: 94.9 us -> 87.2 us
  waiting for transfers between devices: 73 us -> 76.2 us
    pallas_call x1, Pallas kernels: 34.1 us -> 29.4 us  [match_cells(): pl.pallas_call(first_kernel, out_shape=[out_codes, jax.ShapeDtypeStruct((...]
    pallas_call x1, Pallas kernels: 36.4 us -> 33.4 us  [match_cells(): pl.pallas_call(other_kernel, out_shape=out * (CHUNKS - 1), grid_spec=pltp...]
    all_to_all x4, waiting for transfers between devices: 39.4 us -> 42.4 us  [send(): return lax.all_to_all(part, 'patch', 0, 0, tiled=True)]
  transfers between devices with their start and end apart: 17 -> 17, of which waited for: 11 -> 11; matrix products, arithmetic and copies ran while one was open for 2% -> 2% of each run, Pallas kernels for 22% -> 21%
where the time goes in v1:
time: 248 us; the launch traced here: 247 us
  Pallas kernels  87.2 us (35%)
  waiting for transfers between devices  76.2 us (31%)
  starting transfers between devices  45.1 us (18%)
  between operations  16.9 us (7%)
  local copies, waits for them, and re-layouts  16.2 us (7%)
  other arithmetic  4.24 us (2%)
    all_to_all x4, waiting for transfers between devices, send(): return lax.all_to_all(part, 'patch', 0, 0, tiled=True)  42.4 us
    pallas_call x1, Pallas kernels, match_cells(): pl.pallas_call(other_kernel, out_shape=out * (CHUNKS - 1), grid_spec=pltp...  33.4 us
    ppermute x12, waiting for transfers between devices, exchange(): moved.append(lax.ppermute(planes[s], 'exp', ring))  33.1 us
    pallas_call x1, Pallas kernels, match_cells(): pl.pallas_call(first_kernel, out_shape=[out_codes, jax.ShapeDtypeStruct((...  29.4 us
    all_to_all x4, starting transfers between devices, send(): return lax.all_to_all(part, 'patch', 0, 0, tiled=True)  28.7 us
    pallas_call x4, Pallas kernels, add_slots(): pl.pallas_call(functools.partial(add_kernel, begin), out_shape=[share] *...  19.2 us
    ppermute x12, starting transfers between devices, exchange(): moved.append(lax.ppermute(planes[s], 'exp', ring))  16.4 us
    unnamed x42, local copies, waits for them, and re-layouts  9 us
  transfers between devices with their start and end apart: 17, of which 11 were waited for; matrix products, arithmetic and copies ran while one was open for 2% of the time, Pallas kernels for 21%

profile of v1, /device:TPU:1, one launch (start us, length us, event | category | flops | bytes accessed | tf_op | source)
XLA Modules:
  0.0 247.0 jit_solution(5026010383144017344)
XLA Ops:
  14.3 29.4 %match_first.1 = (bf16[32,208,256]{2,1,0:T(8,128)(2,1)S(1)}, bf16[8,32,32,256]{3,2,1,0:T(8,128)(2,1)}, bf16[3,2,32,256]{3,2,1,0:T(8,128)(2,1)}) custom-call(s32[130]{0:T(256)S(1)} %pad_add_fusion.1.dest, bf16[8,512,512]{2,1,0:T(8,128)(2,1)} %img.1, bf16[8,512,512]{2,1,0:T(8,128)(2,1)} %var.3, f32[8,256,1]{2,1,0:T(8,128)S(1)} %broadcast_in_dim_reshape.4.coef, ...), custom_call_target="tpu_custom_call" | custom-call | flops 8999999488 | bytes 30000000 | tf_op jit(solution)/shard_map/match_first/pallas_call | solution.py:298
  45.5 9.6 %all-to-all-start.3 = ((bf16[32,208,256]{2,1,0:T(8,128)(2,1)}), bf16[32,208,256]{2,1,0:T(8,128)(2,1)S(1)}, u32[]{:S(2)}, u32[]{:S(2)}) async-start(bf16[32,208,256]{2,1,0:T(8,128)(2,1)} %copy-done.1), calls=%async_computation.3 | async-start | bytes 6815744 | tf_op jit(solution)/shard_map/all_to_all | solution.py:528
  58.1 33.4 %match_others.1 = (bf16[32,128,256]{2,1,0:T(8,128)(2,1)S(1)}, bf16[32,64,256]{2,1,0:T(8,128)(2,1)}, bf16[32,128,256]{2,1,0:T(8,128)(2,1)S(1)}, bf16[32,64,256]{2...) custom-call(s32[130]{0:T(256)S(1)} %pad_add_fusion.1.dest, ...), custom_call_target="tpu_custom_call" | custom-call | flops 8999999488 | bytes 30000000 | tf_op jit(solution)/shard_map/match_others/pallas_call | solution.py:329
  94.1 3.9 %all-to-all-done.3.got = bf16[32,208,256]{2,1,0:T(8,128)(2,1)S(1)} async-done(((bf16[32,208,256]{2,1,0:T(8,128)(2,1)}), bf16[32,208,256]{2,1,0:T(8,128)(2,1)S(1)}, u32[]{:S(2)}, u32[]{:S(2)}) %all-to-all-start.3) | async-done | bytes 3407904 | tf_op jit(solution)/shard_map/all_to_all | solution.py:528
  98.1 7.7 %all-to-all-start.4 = ((bf16[32,128,256]{2,1,0:T(8,128)(2,1)}), bf16[32,128,256]{2,1,0:T(8,128)(2,1)}, u32[]{:S(2)}, u32[]{:S(2)}) async-start(bf16[32,128,256]{2,1,0:T(8,128)(2,1)} %copy-done.3), calls=%async_computation.4 | async-start | bytes 4194304 | tf_op jit(solution)/shard_map/all_to_all | solution.py:528
  107.5 4.1 %add_slots.10 = (bf16[49,16,256]{2,1,0:T(8,128)(2,1)}, bf16[49,16,256]{2,1,0:T(8,128)(2,1)S(1)}, bf16[49,16,256]{2,1,0:T(8,128)(2,1)}, bf16[49,16,256]{2,1,0:T(8,128)(2,1)S(1)}) custom-call(s32[256]{0:T(256)S(1)} %reshape.362.code, s32[2]{0:T(128)S(1)} %pad_add_fusion.2.group, bf16[32,208,256]{2,1,0:T(8,128)(2,1)S(1)} %all-to-all-done.3.got), custom_call_target="tpu_custom_call" | custom-call | flops 6000000 | bytes 6000000 | tf_op jit(solution)/shard_map/add_slots/pallas_call | solution.py:395
  113.1 26.6 %all-to-all-done.4.got = bf16[32,128,256]{2,1,0:T(8,128)(2,1)} async-done(((bf16[32,128,256]{2,1,0:T(8,128)(2,1)}), bf16[32,128,256]{2,1,0:T(8,128)(2,1)}, u32[]{:S(2)}, u32[]{:S(2)}) %all-to-all-start.4) | async-done | bytes 2097184 | tf_op jit(solution)/shard_map/all_to_all | solution.py:528
  139.7 4.6 %all-to-all-start.6 = ((bf16[32,128,256]{2,1,0:T(8,128)(2,1)}), bf16[32,128,256]{2,1,0:T(8,128)(2,1)S(1)}, u32[]{:S(2)}, u32[]{:S(2)}) async-start(bf16[32,128,256]{2,1,0:T(8,128)(2,1)} %copy-done.2), calls=%async_computation.6 | async-start | bytes 4194304 | tf_op jit(solution)/shard_map/all_to_all | solution.py:528
  144.4 2.8 %collective-permute-start.10 = (bf16[49,16,256]{2,1,0:T(8,128)(2,1)}, bf16[49,16,256]{2,1,0:T(8,128)(2,1)}, u32[]{:S(2)}, u32[]{:S(2)}) collective-permute-start(bf16[49,16,256]{2,1,0:T(8,128)(2,1)} %get-tuple-element.176), channel_id=1, source_target_pairs={{0,64},{32,96},{64,0},{96,32},{1,65},{33,97},{65,1},{97,33},{2,66}... | collective-permute-start | bytes 1204232 | tf_op jit(solution)/shard_map/ppermute | solution.py:478
  148.6 5.5 %add_slots.11 = (bf16[49,16,256]{2,1,0:T(8,128)(2,1)}, bf16[49,16,256]{2,1,0:T(8,128)(2,1)}, bf16[49,16,256]{2,1,0:T(8,128)(2,1)}, bf16[49,16,256]{2,1,0:T(8,128)(2,1)S(1)}) custom-call(s32[256]{0:T(256)S(1)} %reshape.362.code, s32[2]{0:T(128)S(1)} %pad_add_fusion.2.group, bf16[32,128,256]{2,1,0:T(8,128)(2,1)} %all-to-all-done.4.got, ...), custom_call_target="tpu_custom_call" | custom-call | flops 6000000 | bytes 6000000 | tf_op jit(solution)/shard_map/add_slots/pallas_call | solution.py:395
  154.1 2.7 %collective-permute-done.10 = bf16[49,16,256]{2,1,0:T(8,128)(2,1)} collective-permute-done((bf16[49,16,256]{2,1,0:T(8,128)(2,1)}, bf16[49,16,256]{2,1,0:T(8,128)(2,1)}, u32[]{:S(2)}, u32[]{:S(2)}) %collective-permute-start.10) | collective-permute-done | bytes 401440 | tf_op jit(solution)/shard_map/ppermute | solution.py:478
  156.8 8.6 %collective-permute-done.11 = bf16[49,16,256]{2,1,0:T(8,128)(2,1)} collective-permute-done((bf16[49,16,256]{2,1,0:T(8,128)(2,1)S(1)}, bf16[49,16,256]{2,1,0:T(8,128)(2,1)}, u32[]{:S(2)}, u32[]{:S(2)}) %collective-permute-start.11) | collective-permute-done | bytes 401440 | tf_op jit(solution)/shard_map/ppermute | solution.py:478
  166.1 6.2 %all-to-all-done.6.got = bf16[32,128,256]{2,1,0:T(8,128)(2,1)S(1)} async-done(((bf16[32,128,256]{2,1,0:T(8,128)(2,1)}), bf16[32,128,256]{2,1,0:T(8,128)(2,1)S(1)}, u32[]{:S(2)}, u32[]{:S(2)}) %all-to-all-start.6) | async-done | bytes 2097184 | tf_op jit(solution)/shard_map/all_to_all | solution.py:528
  172.3 6.7 %all-to-all-start.5 = ((bf16[32,128,256]{2,1,0:T(8,128)(2,1)}), bf16[32,128,256]{2,1,0:T(8,128)(2,1)}, u32[]{:S(2)}, u32[]{:S(2)}) async-start(bf16[32,128,256]{2,1,0:T(8,128)(2,1)} %get-tuple-element.185), calls=%async_computation.5 | async-start | bytes 4194304 | tf_op jit(solution)/shard_map/all_to_all | solution.py:528
  180.3 2.4 collective-permute-start.13
  183.9 5.1 %add_slots.12 = (bf16[49,16,256]{2,1,0:T(8,128)(2,1)}, bf16[49,16,256]{2,1,0:T(8,128)(2,1)}, bf16[49,16,256]{2,1,0:T(8,128)(2,1)S(1)}, bf16[49,16,256]{2,1,0:T(8,128)(2,1)S(1)}) custom-call(s32[256]{0:T(256)S(1)} %reshape.362.code, s32[2]{0:T(128)S(1)} %pad_add_fusion.2.group, bf16[32,128,256]{2,1,0:T(8,128)(2,1)S(1)} %all-to-all-done.6.got, ...), custom_call_target="tpu_custom_call" | custom-call | flops 6000000 | bytes 6000000 | tf_op jit(solution)/shard_map/add_slots/pallas_call | solution.py:395
  192.4 8.3 %collective-permute-done.13 = bf16[49,16,256]{2,1,0:T(8,128)(2,1)S(1)} collective-permute-done((bf16[49,16,256]{2,1,0:T(8,128)(2,1)}, bf16[49,16,256]{2,1,0:T(8,128)(2,1)S(1)}, u32[]{:S(2)}, u32[]{:S(2)}) %collective-permute-start.13) | collective-permute-done | bytes 401440 | tf_op jit(solution)/shard_map/ppermute | solution.py:478
  201.4 5.6 %all-to-all-done.5.got = bf16[32,128,256]{2,1,0:T(8,128)(2,1)} async-done(((bf16[32,128,256]{2,1,0:T(8,128)(2,1)}), bf16[32,128,256]{2,1,0:T(8,128)(2,1)}, u32[]{:S(2)}, u32[]{:S(2)}) %all-to-all-start.5) | async-done | bytes 2097184 | tf_op jit(solution)/shard_map/all_to_all | solution.py:528
  207.0 4.6 %add_slots.13 = (bf16[49,16,256]{2,1,0:T(8,128)(2,1)S(1)}, bf16[49,16,256]{2,1,0:T(8,128)(2,1)S(1)}, bf16[49,16,256]{2,1,0:T(8,128)(2,1)S(1)}, bf16[49,16,256]{2,1,0:T(8,128)(2,1)S(1)}) custom-call(s32[256]{0:T(256)S(1)} %reshape.362.code, s32[2]{0:T(128)S(1)} %pad_add_fusion.2.group, bf16[32,128,256]{2,1,0:T(8,128)(2,1)} %all-to-all-done.5.got, ...), custom_call_target="tpu_custom_call" | custom-call | flops 6000000 | bytes 6000000 | tf_op jit(solution)/shard_map/add_slots/pallas_call | solution.py:395
  212.9 2.4 collective-permute-start.19
  223.0 4.1 %collective-permute-done.18 = bf16[49,16,256]{2,1,0:T(8,128)(2,1)S(1)} collective-permute-done((bf16[49,16,256]{2,1,0:T(8,128)(2,1)S(1)}, bf16[49,16,256]{2,1,0:T(8,128)(2,1)S(1)}, u32[]{:S(2)}, u32[]{:S(2)}) %collective-permute-start.18) | collective-permute-done | bytes 401440 | tf_op jit(solution)/shard_map/ppermute | solution.py:478
  227.1 7.9 %collective-permute-done.19 = bf16[49,16,256]{2,1,0:T(8,128)(2,1)S(1)} collective-permute-done((bf16[49,16,256]{2,1,0:T(8,128)(2,1)S(1)}, bf16[49,16,256]{2,1,0:T(8,128)(2,1)S(1)}, u32[]{:S(2)}, u32[]{:S(2)}) %collective-permute-start.19) | collective-permute-done | bytes 401440 | tf_op jit(solution)/shard_map/ppermute | solution.py:478
  235.0 5.1 %conditional.1 = (f32[4,6,64,256]{3,2,1,0:T(8,128)}) conditional(s32[]{:T(128)} %bitcast.10, (bf16[49,16,256]{2,1,0:T(8,128)(2,1)S(1)}, bf16[49,16,256]{2,1,0:T(8,128)(2,1)}, bf16[49,16,256]{2,1,0:T(8,128)(2,1)}, bf16[49,16,256]{2,1,0:T(8,128)(2,1)}, bf16[49,16,256]{2,1,0:T(8,128)(2,1)S(1)}, /*index=5*/bf16[49,16,256]{2,1,0:T(8,128)(2,1)S(1)}, ...), branch_computations={%region_7.8_spmd, %region_8.9_spmd} | conditional | flops 18000512 | bytes 59071388 | solution.py:566
  235.0 5.1 %ratio.2 = f32[4,384,256]{2,1,0:T(8,128)} custom-call(bf16[49,16,256]{2,1,0:T(8,128)(2,1)S(1)} %get-tuple-element.82.refs_0_, bf16[49,16,256]{2,1,0:T(8,128)(2,1)} %get-tuple-element.83.refs_1_, bf16[49,16,256]{2,1,0:T(8,128)(2,1)} %get-tuple-element.84.refs_2_, bf16[49,16,256]{2,1,0:T(8,128)(2,1)} %get-tuple-element.85.refs_3_, ...), custom_call_target="tpu_custom_call" | custom-call | tf_op jit(solution)/shard_map/cond/branch_0_fun/ratio/pallas_call | solution.py:444
  (98 shorter events, 32.8 us)
Async XLA Ops:
  12.1 31.6 %copy-start.4 = (f32[8,256,1]{2,1,0:T(8,128)}, f32[8,256,1]{2,1,0:T(8,128)S(1)}, u32[]{:S(2)}) copy-start(f32[8,256,1]{2,1,0:T(8,128)S(1)} %broadcast_in_dim_reshape.4.coef) | copy-start | bytes 24580
  45.5 52.6 %all-to-all-start.3 = ((bf16[32,208,256]{2,1,0:T(8,128)(2,1)}), bf16[32,208,256]{2,1,0:T(8,128)(2,1)S(1)}, u32[]{:S(2)}, u32[]{:S(2)}) async-start(bf16[32,208,256]{2,1,0:T(8,128)(2,1)} %copy-done.1), calls=%async_computation.3 | async-start | bytes 6815744 | tf_op jit(solution)/shard_map/all_to_all | solution.py:528
  55.1 93.5 %all-gather.2.cloned.1.call-start = ((), (), s32[]{:S(2)}) async-start(), calls=%async_computation.7 | async-start | bytes 3244032 | tf_op jit(solution)/shard_map/all_gather | solution.py:530
  98.1 41.6 %all-to-all-start.4 = ((bf16[32,128,256]{2,1,0:T(8,128)(2,1)}), bf16[32,128,256]{2,1,0:T(8,128)(2,1)}, u32[]{:S(2)}, u32[]{:S(2)}) async-start(bf16[32,128,256]{2,1,0:T(8,128)(2,1)} %copy-done.3), calls=%async_computation.4 | async-start | bytes 4194304 | tf_op jit(solution)/shard_map/all_to_all | solution.py:528
  113.1 34.0 %copy-start.14 = (bf16[49,16,256]{2,1,0:T(8,128)(2,1)S(1)}, bf16[49,16,256]{2,1,0:T(8,128)(2,1)}, u32[]{:S(2)}) copy-start(bf16[49,16,256]{2,1,0:T(8,128)(2,1)} %copy-done.13) | copy-start | bytes 1204228
  113.1 34.9 %copy-start.12 = (bf16[49,16,256]{2,1,0:T(8,128)(2,1)S(1)}, bf16[49,16,256]{2,1,0:T(8,128)(2,1)}, u32[]{:S(2)}) copy-start(bf16[49,16,256]{2,1,0:T(8,128)(2,1)} %copy-done.11) | copy-start | bytes 1204228
  139.7 32.6 %all-to-all-start.6 = ((bf16[32,128,256]{2,1,0:T(8,128)(2,1)}), bf16[32,128,256]{2,1,0:T(8,128)(2,1)S(1)}, u32[]{:S(2)}, u32[]{:S(2)}) async-start(bf16[32,128,256]{2,1,0:T(8,128)(2,1)} %copy-done.2), calls=%async_computation.6 | async-start | bytes 4194304 | tf_op jit(solution)/shard_map/all_to_all | solution.py:528
  144.4 12.5 %collective-permute-start.10 = (bf16[49,16,256]{2,1,0:T(8,128)(2,1)}, bf16[49,16,256]{2,1,0:T(8,128)(2,1)}, u32[]{:S(2)}, u32[]{:S(2)}) collective-permute-start(bf16[49,16,256]{2,1,0:T(8,128)(2,1)} %get-tuple-element.176), channel_id=1, source_target_pairs={{0,64},{32,96},{64,0},{96,32},{1,65},{33,97},{65,1},{97,33},{2,66}... | collective-permute-start | bytes 1204232 | tf_op jit(solution)/shard_map/ppermute | solution.py:478
  147.1 18.3 %collective-permute-start.11 = (bf16[49,16,256]{2,1,0:T(8,128)(2,1)S(1)}, bf16[49,16,256]{2,1,0:T(8,128)(2,1)}, u32[]{:S(2)}, u32[]{:S(2)}) collective-permute-start(bf16[49,16,256]{2,1,0:T(8,128)(2,1)S(1)} %copy-done.14), channel_id=1, source_target_pairs={{0,96},{32,0},{64,32},{96,64},{1,97},{33,1},{65,33},{97,65},{2,98}... | collective-permute-start | bytes 1204232 | tf_op jit(solution)/shard_map/ppermute | solution.py:478
  148.0 18.0 %collective-permute-start.9 = (bf16[49,16,256]{2,1,0:T(8,128)(2,1)S(1)}, bf16[49,16,256]{2,1,0:T(8,128)(2,1)}, u32[]{:S(2)}, u32[]{:S(2)}) collective-permute-start(bf16[49,16,256]{2,1,0:T(8,128)(2,1)S(1)} %copy-done.12), channel_id=1, source_target_pairs={{0,32},{32,64},{64,96},{96,0},{1,33},{33,65},{65,97},{97,1},{2,34}... | collective-permute-start | bytes 1204232 | tf_op jit(solution)/shard_map/ppermute | solution.py:478
  172.3 34.7 %all-to-all-start.5 = ((bf16[32,128,256]{2,1,0:T(8,128)(2,1)}), bf16[32,128,256]{2,1,0:T(8,128)(2,1)}, u32[]{:S(2)}, u32[]{:S(2)}) async-start(bf16[32,128,256]{2,1,0:T(8,128)(2,1)} %get-tuple-element.185), calls=%async_computation.5 | async-start | bytes 4194304 | tf_op jit(solution)/shard_map/all_to_all | solution.py:528
  179.0 12.0 %collective-permute-start.12 = (bf16[49,16,256]{2,1,0:T(8,128)(2,1)}, bf16[49,16,256]{2,1,0:T(8,128)(2,1)S(1)}, u32[]{:S(2)}, u32[]{:S(2)}) collective-permute-start(bf16[49,16,256]{2,1,0:T(8,128)(2,1)} %get-tuple-element.187), channel_id=1, source_target_pairs={{0,32},{32,64},{64,96},{96,0},{1,33},{33,65},{65,97},{97,1},{2,34}... | collective-permute-start | bytes 1204232 | tf_op jit(solution)/shard_map/ppermute | solution.py:478
  180.3 20.3 %collective-permute-start.13 = (bf16[49,16,256]{2,1,0:T(8,128)(2,1)}, bf16[49,16,256]{2,1,0:T(8,128)(2,1)S(1)}, u32[]{:S(2)}, u32[]{:S(2)}) collective-permute-start(bf16[49,16,256]{2,1,0:T(8,128)(2,1)} %get-tuple-element.188), channel_id=1, source_target_pairs={{0,64},{32,96},{64,0},{96,32},{1,65},{33,97},{65,1},{97,33},{2,66}... | collective-permute-start | bytes 1204232 | tf_op jit(solution)/shard_map/ppermute | solution.py:478
  182.7 18.7 %collective-permute-start.14 = (bf16[49,16,256]{2,1,0:T(8,128)(2,1)S(1)}, bf16[49,16,256]{2,1,0:T(8,128)(2,1)}, u32[]{:S(2)}, u32[]{:S(2)}) collective-permute-start(bf16[49,16,256]{2,1,0:T(8,128)(2,1)S(1)} %get-tuple-element.189), channel_id=1, source_target_pairs={{0,96},{32,0},{64,32},{96,64},{1,97},{33,1},{65,33},{97,65},{2,98}... | collective-permute-start | bytes 1204232 | tf_op jit(solution)/shard_map/ppermute | solution.py:478
  188.9 26.3 %collective-permute-start.15 = (bf16[49,16,256]{2,1,0:T(8,128)(2,1)}, bf16[49,16,256]{2,1,0:T(8,128)(2,1)}, u32[]{:S(2)}, u32[]{:S(2)}) collective-permute-start(bf16[49,16,256]{2,1,0:T(8,128)(2,1)} %get-tuple-element.196), channel_id=1, source_target_pairs={{0,32},{32,64},{64,96},{96,0},{1,33},{33,65},{65,97},{97,1},{2,34}... | collective-permute-start | bytes 1204232 | tf_op jit(solution)/shard_map/ppermute | solution.py:478
  189.2 33.8 %collective-permute-start.16 = (bf16[49,16,256]{2,1,0:T(8,128)(2,1)S(1)}, bf16[49,16,256]{2,1,0:T(8,128)(2,1)}, u32[]{:S(2)}, u32[]{:S(2)}) collective-permute-start(bf16[49,16,256]{2,1,0:T(8,128)(2,1)S(1)} %get-tuple-element.197), channel_id=1, source_target_pairs={{0,64},{32,96},{64,0},{96,32},{1,65},{33,97},{65,1},{97,33},{2,66}... | collective-permute-start | bytes 1204232 | tf_op jit(solution)/shard_map/ppermute | solution.py:478
  191.1 43.9 %copy-start.17 = (bf16[49,16,256]{2,1,0:T(8,128)(2,1)S(1)}, bf16[49,16,256]{2,1,0:T(8,128)(2,1)}, u32[]{:S(2)}) copy-start(bf16[49,16,256]{2,1,0:T(8,128)(2,1)} %get-tuple-element.190) | copy-start | bytes 1204228
  191.1 43.9 %copy-start.25 = (bf16[49,16,256]{2,1,0:T(8,128)(2,1)S(1)}, bf16[49,16,256]{2,1,0:T(8,128)(2,1)}, u32[]{:S(2)}) copy-start(bf16[49,16,256]{2,1,0:T(8,128)(2,1)} %get-tuple-element.195) | copy-start | bytes 1204228
  191.1 31.9 %collective-permute-start.17 = (bf16[49,16,256]{2,1,0:T(8,128)(2,1)S(1)}, bf16[49,16,256]{2,1,0:T(8,128)(2,1)}, u32[]{:S(2)}, u32[]{:S(2)}) collective-permute-start(bf16[49,16,256]{2,1,0:T(8,128)(2,1)S(1)} %get-tuple-element.198), channel_id=1, source_target_pairs={{0,96},{32,0},{64,32},{96,64},{1,97},{33,1},{65,33},{97,65},{2,98}... | collective-permute-start | bytes 1204232 | tf_op jit(solution)/shard_map/ppermute | solution.py:478
  201.4 33.6 %copy-start.20 = (bf16[49,16,256]{2,1,0:T(8,128)(2,1)S(1)}, bf16[49,16,256]{2,1,0:T(8,128)(2,1)}, u32[]{:S(2)}) copy-start(bf16[49,16,256]{2,1,0:T(8,128)(2,1)} %copy-done.19) | copy-start | bytes 1204228
  201.4 33.6 %copy-start.23 = (bf16[49,16,256]{2,1,0:T(8,128)(2,1)S(1)}, bf16[49,16,256]{2,1,0:T(8,128)(2,1)}, u32[]{:S(2)}) copy-start(bf16[49,16,256]{2,1,0:T(8,128)(2,1)} %copy-done.22) | copy-start | bytes 1204228
  211.6 15.5 %collective-permute-start.18 = (bf16[49,16,256]{2,1,0:T(8,128)(2,1)S(1)}, bf16[49,16,256]{2,1,0:T(8,128)(2,1)S(1)}, u32[]{:S(2)}, u32[]{:S(2)}) collective-permute-start(bf16[49,16,256]{2,1,0:T(8,128)(2,1)S(1)} %get-tuple-element.201), channel_id=1, source_target_pairs={{0,32},{32,64},{64,96},{96,0},{1,33},{33,65},{65,97},{97,1},{2,34}... | collective-permute-start | bytes 1204232 | tf_op jit(solution)/shard_map/ppermute | solution.py:478
  212.9 22.1 %collective-permute-start.19 = (bf16[49,16,256]{2,1,0:T(8,128)(2,1)S(1)}, bf16[49,16,256]{2,1,0:T(8,128)(2,1)S(1)}, u32[]{:S(2)}, u32[]{:S(2)}) collective-permute-start(bf16[49,16,256]{2,1,0:T(8,128)(2,1)S(1)} %get-tuple-element.202), channel_id=1, source_target_pairs={{0,64},{32,96},{64,0},{96,32},{1,65},{33,97},{65,1},{97,33},{2,66}... | collective-permute-start | bytes 1204232 | tf_op jit(solution)/shard_map/ppermute | solution.py:478
  215.3 19.7 %collective-permute-start.20 = (bf16[49,16,256]{2,1,0:T(8,128)(2,1)S(1)}, bf16[49,16,256]{2,1,0:T(8,128)(2,1)S(1)}, u32[]{:S(2)}, u32[]{:S(2)}) collective-permute-start(bf16[49,16,256]{2,1,0:T(8,128)(2,1)S(1)} %get-tuple-element.203), channel_id=1, source_target_pairs={{0,96},{32,0},{64,32},{96,64},{1,97},{33,1},{65,33},{97,65},{2,98}... | collective-permute-start | bytes 1204232 | tf_op jit(solution)/shard_map/ppermute | solution.py:478
  (14 other events, 128.5 us)
Sparse Core Ops, SparseCore 0:
  58.2 76.2 all-gather.1

commit v2 on v1

--- a/solution.py
+++ b/solution.py
@@ -365,7 +365,7 @@
 
         return 0
 
-    lax.fori_loop(0, per, one, 0)
+    lax.fori_loop(0, per, one, 0, unroll=2)
 
     @pl.when(step == pl.num_programs(0) - 1)
     def _():
@@ -379,7 +379,7 @@
                 out[p] = part.reshape(16, 256).astype(BF16)
             return 0
 
-        lax.fori_loop(0, 48, put, 0, unroll=2)
+        lax.fori_loop(0, 48, put, 0, unroll=4)
         for out in outs:
             out[48] = jnp.full((16, 256), group[1].astype(F32), F32).astype(BF16)
 

time: 248 us -> 248 us (level)
  no operation moved by 1% of the time
where the time goes in v2:
time: 248 us; the launch traced here: 247 us
  Pallas kernels  86.3 us (35%)
  waiting for transfers between devices  77 us (31%)
  starting transfers between devices  45.1 us (18%)
  between operations  16.9 us (7%)
  local copies, waits for them, and re-layouts  16.2 us (7%)
  other arithmetic  4.24 us (2%)
    all_to_all x4, waiting for transfers between devices, send(): return lax.all_to_all(part, 'patch', 0, 0, tiled=True)  42.5 us
    ppermute x12, waiting for transfers between devices, exchange(): moved.append(lax.ppermute(planes[s], 'exp', ring))  33.9 us
    pallas_call x1, Pallas kernels, match_cells(): pl.pallas_call(other_kernel, out_shape=out * (CHUNKS - 1), grid_spec=pltp...  33.4 us
    pallas_call x1, Pallas kernels, match_cells(): pl.pallas_call(first_kernel, out_shape=[out_codes, jax.ShapeDtypeStruct((...  29.4 us
    all_to_all x4, starting transfers between devices, send(): return lax.all_to_all(part, 'patch', 0, 0, tiled=True)  28.7 us
    pallas_call x4, Pallas kernels, add_slots(): pl.pallas_call(functools.partial(add_kernel, begin), out_shape=[share] *...  18.4 us
    ppermute x12, starting transfers between devices, exchange(): moved.append(lax.ppermute(planes[s], 'exp', ring))  16.3 us
    unnamed x42, local copies, waits for them, and re-layouts  9 us
  transfers between devices with their start and end apart: 17, of which 11 were waited for; matrix products, arithmetic and copies ran while one was open for 2% of the time, Pallas kernels for 21%

profile of v2, /device:TPU:1, one launch (start us, length us, event | category | flops | bytes accessed | tf_op | source)
XLA Modules:
  0.0 247.0 jit_solution(3373112449486871680)
XLA Ops:
  14.3 29.4 %match_first.1 = (bf16[32,208,256]{2,1,0:T(8,128)(2,1)S(1)}, bf16[8,32,32,256]{3,2,1,0:T(8,128)(2,1)}, bf16[3,2,32,256]{3,2,1,0:T(8,128)(2,1)}) custom-call(s32[130]{0:T(256)S(1)} %pad_add_fusion.1.dest, bf16[8,512,512]{2,1,0:T(8,128)(2,1)} %img.1, bf16[8,512,512]{2,1,0:T(8,128)(2,1)} %var.3, f32[8,256,1]{2,1,0:T(8,128)S(1)} %broadcast_in_dim_reshape.4.coef, ...), custom_call_target="tpu_custom_call" | custom-call | flops 8999999488 | bytes 30000000 | tf_op jit(solution)/shard_map/match_first/pallas_call | solution.py:298
  45.5 9.6 %all-to-all-start.3 = ((bf16[32,208,256]{2,1,0:T(8,128)(2,1)}), bf16[32,208,256]{2,1,0:T(8,128)(2,1)S(1)}, u32[]{:S(2)}, u32[]{:S(2)}) async-start(bf16[32,208,256]{2,1,0:T(8,128)(2,1)} %copy-done.1), calls=%async_computation.3 | async-start | bytes 6815744 | tf_op jit(solution)/shard_map/all_to_all | solution.py:528
  58.1 33.4 %match_others.1 = (bf16[32,128,256]{2,1,0:T(8,128)(2,1)S(1)}, bf16[32,64,256]{2,1,0:T(8,128)(2,1)}, bf16[32,128,256]{2,1,0:T(8,128)(2,1)S(1)}, bf16[32,64,256]{2...) custom-call(s32[130]{0:T(256)S(1)} %pad_add_fusion.1.dest, ...), custom_call_target="tpu_custom_call" | custom-call | flops 8999999488 | bytes 30000000 | tf_op jit(solution)/shard_map/match_others/pallas_call | solution.py:329
  94.2 3.9 %all-to-all-done.3.got = bf16[32,208,256]{2,1,0:T(8,128)(2,1)S(1)} async-done(((bf16[32,208,256]{2,1,0:T(8,128)(2,1)}), bf16[32,208,256]{2,1,0:T(8,128)(2,1)S(1)}, u32[]{:S(2)}, u32[]{:S(2)}) %all-to-all-start.3) | async-done | bytes 3407904 | tf_op jit(solution)/shard_map/all_to_all | solution.py:528
  98.1 7.7 %all-to-all-start.4 = ((bf16[32,128,256]{2,1,0:T(8,128)(2,1)}), bf16[32,128,256]{2,1,0:T(8,128)(2,1)}, u32[]{:S(2)}, u32[]{:S(2)}) async-start(bf16[32,128,256]{2,1,0:T(8,128)(2,1)} %copy-done.3), calls=%async_computation.4 | async-start | bytes 4194304 | tf_op jit(solution)/shard_map/all_to_all | solution.py:528
  107.5 3.9 %add_slots.10 = (bf16[49,16,256]{2,1,0:T(8,128)(2,1)}, bf16[49,16,256]{2,1,0:T(8,128)(2,1)S(1)}, bf16[49,16,256]{2,1,0:T(8,128)(2,1)}, bf16[49,16,256]{2,1,0:T(8,128)(2,1)S(1)}) custom-call(s32[256]{0:T(256)S(1)} %reshape.362.code, s32[2]{0:T(128)S(1)} %pad_add_fusion.2.group, bf16[32,208,256]{2,1,0:T(8,128)(2,1)S(1)} %all-to-all-done.3.got), custom_call_target="tpu_custom_call" | custom-call | flops 6000000 | bytes 6000000 | tf_op jit(solution)/shard_map/add_slots/pallas_call | solution.py:395
  113.0 26.7 %all-to-all-done.4.got = bf16[32,128,256]{2,1,0:T(8,128)(2,1)} async-done(((bf16[32,128,256]{2,1,0:T(8,128)(2,1)}), bf16[32,128,256]{2,1,0:T(8,128)(2,1)}, u32[]{:S(2)}, u32[]{:S(2)}) %all-to-all-start.4) | async-done | bytes 2097184 | tf_op jit(solution)/shard_map/all_to_all | solution.py:528
  139.7 4.6 %all-to-all-start.6 = ((bf16[32,128,256]{2,1,0:T(8,128)(2,1)}), bf16[32,128,256]{2,1,0:T(8,128)(2,1)S(1)}, u32[]{:S(2)}, u32[]{:S(2)}) async-start(bf16[32,128,256]{2,1,0:T(8,128)(2,1)} %copy-done.2), calls=%async_computation.6 | async-start | bytes 4194304 | tf_op jit(solution)/shard_map/all_to_all | solution.py:528
  144.4 2.8 %collective-permute-start.10 = (bf16[49,16,256]{2,1,0:T(8,128)(2,1)}, bf16[49,16,256]{2,1,0:T(8,128)(2,1)}, u32[]{:S(2)}, u32[]{:S(2)}) collective-permute-start(bf16[49,16,256]{2,1,0:T(8,128)(2,1)} %get-tuple-element.176), channel_id=1, source_target_pairs={{0,64},{32,96},{64,0},{96,32},{1,65},{33,97},{65,1},{97,33},{2,66}... | collective-permute-start | bytes 1204232 | tf_op jit(solution)/shard_map/ppermute | solution.py:478
  148.6 5.3 %add_slots.11 = (bf16[49,16,256]{2,1,0:T(8,128)(2,1)}, bf16[49,16,256]{2,1,0:T(8,128)(2,1)}, bf16[49,16,256]{2,1,0:T(8,128)(2,1)}, bf16[49,16,256]{2,1,0:T(8,128)(2,1)S(1)}) custom-call(s32[256]{0:T(256)S(1)} %reshape.362.code, s32[2]{0:T(128)S(1)} %pad_add_fusion.2.group, bf16[32,128,256]{2,1,0:T(8,128)(2,1)} %all-to-all-done.4.got, ...), custom_call_target="tpu_custom_call" | custom-call | flops 6000000 | bytes 6000000 | tf_op jit(solution)/shard_map/add_slots/pallas_call | solution.py:395
  153.9 2.9 %collective-permute-done.10 = bf16[49,16,256]{2,1,0:T(8,128)(2,1)} collective-permute-done((bf16[49,16,256]{2,1,0:T(8,128)(2,1)}, bf16[49,16,256]{2,1,0:T(8,128)(2,1)}, u32[]{:S(2)}, u32[]{:S(2)}) %collective-permute-start.10) | collective-permute-done | bytes 401440 | tf_op jit(solution)/shard_map/ppermute | solution.py:478
  156.8 8.6 %collective-permute-done.11 = bf16[49,16,256]{2,1,0:T(8,128)(2,1)} collective-permute-done((bf16[49,16,256]{2,1,0:T(8,128)(2,1)S(1)}, bf16[49,16,256]{2,1,0:T(8,128)(2,1)}, u32[]{:S(2)}, u32[]{:S(2)}) %collective-permute-start.11) | collective-permute-done | bytes 401440 | tf_op jit(solution)/shard_map/ppermute | solution.py:478
  166.1 6.2 %all-to-all-done.6.got = bf16[32,128,256]{2,1,0:T(8,128)(2,1)S(1)} async-done(((bf16[32,128,256]{2,1,0:T(8,128)(2,1)}), bf16[32,128,256]{2,1,0:T(8,128)(2,1)S(1)}, u32[]{:S(2)}, u32[]{:S(2)}) %all-to-all-start.6) | async-done | bytes 2097184 | tf_op jit(solution)/shard_map/all_to_all | solution.py:528
  172.3 6.7 %all-to-all-start.5 = ((bf16[32,128,256]{2,1,0:T(8,128)(2,1)}), bf16[32,128,256]{2,1,0:T(8,128)(2,1)}, u32[]{:S(2)}, u32[]{:S(2)}) async-start(bf16[32,128,256]{2,1,0:T(8,128)(2,1)} %get-tuple-element.185), calls=%async_computation.5 | async-start | bytes 4194304 | tf_op jit(solution)/shard_map/all_to_all | solution.py:528
  180.3 2.4 collective-permute-start.13
  183.9 4.8 %add_slots.12 = (bf16[49,16,256]{2,1,0:T(8,128)(2,1)}, bf16[49,16,256]{2,1,0:T(8,128)(2,1)}, bf16[49,16,256]{2,1,0:T(8,128)(2,1)S(1)}, bf16[49,16,256]{2,1,0:T(8,128)(2,1)S(1)}) custom-call(s32[256]{0:T(256)S(1)} %reshape.362.code, s32[2]{0:T(128)S(1)} %pad_add_fusion.2.group, bf16[32,128,256]{2,1,0:T(8,128)(2,1)S(1)} %all-to-all-done.6.got, ...), custom_call_target="tpu_custom_call" | custom-call | flops 6000000 | bytes 6000000 | tf_op jit(solution)/shard_map/add_slots/pallas_call | solution.py:395
  192.4 8.3 %collective-permute-done.13 = bf16[49,16,256]{2,1,0:T(8,128)(2,1)S(1)} collective-permute-done((bf16[49,16,256]{2,1,0:T(8,128)(2,1)}, bf16[49,16,256]{2,1,0:T(8,128)(2,1)S(1)}, u32[]{:S(2)}, u32[]{:S(2)}) %collective-permute-start.13) | collective-permute-done | bytes 401440 | tf_op jit(solution)/shard_map/ppermute | solution.py:478
  201.4 5.6 %all-to-all-done.5.got = bf16[32,128,256]{2,1,0:T(8,128)(2,1)} async-done(((bf16[32,128,256]{2,1,0:T(8,128)(2,1)}), bf16[32,128,256]{2,1,0:T(8,128)(2,1)}, u32[]{:S(2)}, u32[]{:S(2)}) %all-to-all-start.5) | async-done | bytes 2097184 | tf_op jit(solution)/shard_map/all_to_all | solution.py:528
  207.0 4.3 %add_slots.13 = (bf16[49,16,256]{2,1,0:T(8,128)(2,1)S(1)}, bf16[49,16,256]{2,1,0:T(8,128)(2,1)S(1)}, bf16[49,16,256]{2,1,0:T(8,128)(2,1)S(1)}, bf16[49,16,256]{2,1,0:T(8,128)(2,1)S(1)}) custom-call(s32[256]{0:T(256)S(1)} %reshape.362.code, s32[2]{0:T(128)S(1)} %pad_add_fusion.2.group, bf16[32,128,256]{2,1,0:T(8,128)(2,1)} %all-to-all-done.5.got, ...), custom_call_target="tpu_custom_call" | custom-call | flops 6000000 | bytes 6000000 | tf_op jit(solution)/shard_map/add_slots/pallas_call | solution.py:395
  212.6 2.4 collective-permute-start.19
  222.8 4.7 %collective-permute-done.18 = bf16[49,16,256]{2,1,0:T(8,128)(2,1)S(1)} collective-permute-done((bf16[49,16,256]{2,1,0:T(8,128)(2,1)S(1)}, bf16[49,16,256]{2,1,0:T(8,128)(2,1)S(1)}, u32[]{:S(2)}, u32[]{:S(2)}) %collective-permute-start.18) | collective-permute-done | bytes 401440 | tf_op jit(solution)/shard_map/ppermute | solution.py:478
  227.5 7.5 %collective-permute-done.19 = bf16[49,16,256]{2,1,0:T(8,128)(2,1)S(1)} collective-permute-done((bf16[49,16,256]{2,1,0:T(8,128)(2,1)S(1)}, bf16[49,16,256]{2,1,0:T(8,128)(2,1)S(1)}, u32[]{:S(2)}, u32[]{:S(2)}) %collective-permute-start.19) | collective-permute-done | bytes 401440 | tf_op jit(solution)/shard_map/ppermute | solution.py:478
  235.0 5.1 %conditional.1 = (f32[4,6,64,256]{3,2,1,0:T(8,128)}) conditional(s32[]{:T(128)} %bitcast.10, (bf16[49,16,256]{2,1,0:T(8,128)(2,1)S(1)}, bf16[49,16,256]{2,1,0:T(8,128)(2,1)}, bf16[49,16,256]{2,1,0:T(8,128)(2,1)}, bf16[49,16,256]{2,1,0:T(8,128)(2,1)}, bf16[49,16,256]{2,1,0:T(8,128)(2,1)S(1)}, /*index=5*/bf16[49,16,256]{2,1,0:T(8,128)(2,1)S(1)}, ...), branch_computations={%region_7.8_spmd, %region_8.9_spmd} | conditional | flops 18000512 | bytes 59071388 | solution.py:566
  235.0 5.1 %ratio.2 = f32[4,384,256]{2,1,0:T(8,128)} custom-call(bf16[49,16,256]{2,1,0:T(8,128)(2,1)S(1)} %get-tuple-element.82.refs_0_, bf16[49,16,256]{2,1,0:T(8,128)(2,1)} %get-tuple-element.83.refs_1_, bf16[49,16,256]{2,1,0:T(8,128)(2,1)} %get-tuple-element.84.refs_2_, bf16[49,16,256]{2,1,0:T(8,128)(2,1)} %get-tuple-element.85.refs_3_, ...), custom_call_target="tpu_custom_call" | custom-call | tf_op jit(solution)/shard_map/cond/branch_0_fun/ratio/pallas_call | solution.py:444
  (98 shorter events, 33.1 us)
Async XLA Ops:
  12.1 31.6 %copy-start.4 = (f32[8,256,1]{2,1,0:T(8,128)}, f32[8,256,1]{2,1,0:T(8,128)S(1)}, u32[]{:S(2)}) copy-start(f32[8,256,1]{2,1,0:T(8,128)S(1)} %broadcast_in_dim_reshape.4.coef) | copy-start | bytes 24580
  45.5 52.6 %all-to-all-start.3 = ((bf16[32,208,256]{2,1,0:T(8,128)(2,1)}), bf16[32,208,256]{2,1,0:T(8,128)(2,1)S(1)}, u32[]{:S(2)}, u32[]{:S(2)}) async-start(bf16[32,208,256]{2,1,0:T(8,128)(2,1)} %copy-done.1), calls=%async_computation.3 | async-start | bytes 6815744 | tf_op jit(solution)/shard_map/all_to_all | solution.py:528
  55.1 93.5 %all-gather.2.cloned.1.call-start = ((), (), s32[]{:S(2)}) async-start(), calls=%async_computation.7 | async-start | bytes 3244032 | tf_op jit(solution)/shard_map/all_gather | solution.py:530
  98.1 41.6 %all-to-all-start.4 = ((bf16[32,128,256]{2,1,0:T(8,128)(2,1)}), bf16[32,128,256]{2,1,0:T(8,128)(2,1)}, u32[]{:S(2)}, u32[]{:S(2)}) async-start(bf16[32,128,256]{2,1,0:T(8,128)(2,1)} %copy-done.3), calls=%async_computation.4 | async-start | bytes 4194304 | tf_op jit(solution)/shard_map/all_to_all | solution.py:528
  113.0 34.2 %copy-start.14 = (bf16[49,16,256]{2,1,0:T(8,128)(2,1)S(1)}, bf16[49,16,256]{2,1,0:T(8,128)(2,1)}, u32[]{:S(2)}) copy-start(bf16[49,16,256]{2,1,0:T(8,128)(2,1)} %copy-done.13) | copy-start | bytes 1204228
  113.0 35.1 %copy-start.12 = (bf16[49,16,256]{2,1,0:T(8,128)(2,1)S(1)}, bf16[49,16,256]{2,1,0:T(8,128)(2,1)}, u32[]{:S(2)}) copy-start(bf16[49,16,256]{2,1,0:T(8,128)(2,1)} %copy-done.11) | copy-start | bytes 1204228
  139.7 32.6 %all-to-all-start.6 = ((bf16[32,128,256]{2,1,0:T(8,128)(2,1)}), bf16[32,128,256]{2,1,0:T(8,128)(2,1)S(1)}, u32[]{:S(2)}, u32[]{:S(2)}) async-start(bf16[32,128,256]{2,1,0:T(8,128)(2,1)} %copy-done.2), calls=%async_computation.6 | async-start | bytes 4194304 | tf_op jit(solution)/shard_map/all_to_all | solution.py:528
  144.4 12.5 %collective-permute-start.10 = (bf16[49,16,256]{2,1,0:T(8,128)(2,1)}, bf16[49,16,256]{2,1,0:T(8,128)(2,1)}, u32[]{:S(2)}, u32[]{:S(2)}) collective-permute-start(bf16[49,16,256]{2,1,0:T(8,128)(2,1)} %get-tuple-element.176), channel_id=1, source_target_pairs={{0,64},{32,96},{64,0},{96,32},{1,65},{33,97},{65,1},{97,33},{2,66}... | collective-permute-start | bytes 1204232 | tf_op jit(solution)/shard_map/ppermute | solution.py:478
  147.1 18.3 %collective-permute-start.11 = (bf16[49,16,256]{2,1,0:T(8,128)(2,1)S(1)}, bf16[49,16,256]{2,1,0:T(8,128)(2,1)}, u32[]{:S(2)}, u32[]{:S(2)}) collective-permute-start(bf16[49,16,256]{2,1,0:T(8,128)(2,1)S(1)} %copy-done.14), channel_id=1, source_target_pairs={{0,96},{32,0},{64,32},{96,64},{1,97},{33,1},{65,33},{97,65},{2,98}... | collective-permute-start | bytes 1204232 | tf_op jit(solution)/shard_map/ppermute | solution.py:478
  148.0 18.0 %collective-permute-start.9 = (bf16[49,16,256]{2,1,0:T(8,128)(2,1)S(1)}, bf16[49,16,256]{2,1,0:T(8,128)(2,1)}, u32[]{:S(2)}, u32[]{:S(2)}) collective-permute-start(bf16[49,16,256]{2,1,0:T(8,128)(2,1)S(1)} %copy-done.12), channel_id=1, source_target_pairs={{0,32},{32,64},{64,96},{96,0},{1,33},{33,65},{65,97},{97,1},{2,34}... | collective-permute-start | bytes 1204232 | tf_op jit(solution)/shard_map/ppermute | solution.py:478
  172.3 34.7 %all-to-all-start.5 = ((bf16[32,128,256]{2,1,0:T(8,128)(2,1)}), bf16[32,128,256]{2,1,0:T(8,128)(2,1)}, u32[]{:S(2)}, u32[]{:S(2)}) async-start(bf16[32,128,256]{2,1,0:T(8,128)(2,1)} %get-tuple-element.185), calls=%async_computation.5 | async-start | bytes 4194304 | tf_op jit(solution)/shard_map/all_to_all | solution.py:528
  179.0 12.0 %collective-permute-start.12 = (bf16[49,16,256]{2,1,0:T(8,128)(2,1)}, bf16[49,16,256]{2,1,0:T(8,128)(2,1)S(1)}, u32[]{:S(2)}, u32[]{:S(2)}) collective-permute-start(bf16[49,16,256]{2,1,0:T(8,128)(2,1)} %get-tuple-element.187), channel_id=1, source_target_pairs={{0,32},{32,64},{64,96},{96,0},{1,33},{33,65},{65,97},{97,1},{2,34}... | collective-permute-start | bytes 1204232 | tf_op jit(solution)/shard_map/ppermute | solution.py:478
  180.3 20.3 %collective-permute-start.13 = (bf16[49,16,256]{2,1,0:T(8,128)(2,1)}, bf16[49,16,256]{2,1,0:T(8,128)(2,1)S(1)}, u32[]{:S(2)}, u32[]{:S(2)}) collective-permute-start(bf16[49,16,256]{2,1,0:T(8,128)(2,1)} %get-tuple-element.188), channel_id=1, source_target_pairs={{0,64},{32,96},{64,0},{96,32},{1,65},{33,97},{65,1},{97,33},{2,66}... | collective-permute-start | bytes 1204232 | tf_op jit(solution)/shard_map/ppermute | solution.py:478
  182.7 18.7 %collective-permute-start.14 = (bf16[49,16,256]{2,1,0:T(8,128)(2,1)S(1)}, bf16[49,16,256]{2,1,0:T(8,128)(2,1)}, u32[]{:S(2)}, u32[]{:S(2)}) collective-permute-start(bf16[49,16,256]{2,1,0:T(8,128)(2,1)S(1)} %get-tuple-element.189), channel_id=1, source_target_pairs={{0,96},{32,0},{64,32},{96,64},{1,97},{33,1},{65,33},{97,65},{2,98}... | collective-permute-start | bytes 1204232 | tf_op jit(solution)/shard_map/ppermute | solution.py:478
  188.7 26.3 %collective-permute-start.15 = (bf16[49,16,256]{2,1,0:T(8,128)(2,1)}, bf16[49,16,256]{2,1,0:T(8,128)(2,1)}, u32[]{:S(2)}, u32[]{:S(2)}) collective-permute-start(bf16[49,16,256]{2,1,0:T(8,128)(2,1)} %get-tuple-element.196), channel_id=1, source_target_pairs={{0,32},{32,64},{64,96},{96,0},{1,33},{33,65},{65,97},{97,1},{2,34}... | collective-permute-start | bytes 1204232 | tf_op jit(solution)/shard_map/ppermute | solution.py:478
  188.9 33.8 %collective-permute-start.16 = (bf16[49,16,256]{2,1,0:T(8,128)(2,1)S(1)}, bf16[49,16,256]{2,1,0:T(8,128)(2,1)}, u32[]{:S(2)}, u32[]{:S(2)}) collective-permute-start(bf16[49,16,256]{2,1,0:T(8,128)(2,1)S(1)} %get-tuple-element.197), channel_id=1, source_target_pairs={{0,64},{32,96},{64,0},{96,32},{1,65},{33,97},{65,1},{97,33},{2,66}... | collective-permute-start | bytes 1204232 | tf_op jit(solution)/shard_map/ppermute | solution.py:478
  191.1 43.9 %copy-start.17 = (bf16[49,16,256]{2,1,0:T(8,128)(2,1)S(1)}, bf16[49,16,256]{2,1,0:T(8,128)(2,1)}, u32[]{:S(2)}) copy-start(bf16[49,16,256]{2,1,0:T(8,128)(2,1)} %get-tuple-element.190) | copy-start | bytes 1204228
  191.1 43.9 %copy-start.25 = (bf16[49,16,256]{2,1,0:T(8,128)(2,1)S(1)}, bf16[49,16,256]{2,1,0:T(8,128)(2,1)}, u32[]{:S(2)}) copy-start(bf16[49,16,256]{2,1,0:T(8,128)(2,1)} %get-tuple-element.195) | copy-start | bytes 1204228
  191.1 31.7 %collective-permute-start.17 = (bf16[49,16,256]{2,1,0:T(8,128)(2,1)S(1)}, bf16[49,16,256]{2,1,0:T(8,128)(2,1)}, u32[]{:S(2)}, u32[]{:S(2)}) collective-permute-start(bf16[49,16,256]{2,1,0:T(8,128)(2,1)S(1)} %get-tuple-element.198), channel_id=1, source_target_pairs={{0,96},{32,0},{64,32},{96,64},{1,97},{33,1},{65,33},{97,65},{2,98}... | collective-permute-start | bytes 1204232 | tf_op jit(solution)/shard_map/ppermute | solution.py:478
  201.4 33.6 %copy-start.20 = (bf16[49,16,256]{2,1,0:T(8,128)(2,1)S(1)}, bf16[49,16,256]{2,1,0:T(8,128)(2,1)}, u32[]{:S(2)}) copy-start(bf16[49,16,256]{2,1,0:T(8,128)(2,1)} %copy-done.19) | copy-start | bytes 1204228
  201.4 33.6 %copy-start.23 = (bf16[49,16,256]{2,1,0:T(8,128)(2,1)S(1)}, bf16[49,16,256]{2,1,0:T(8,128)(2,1)}, u32[]{:S(2)}) copy-start(bf16[49,16,256]{2,1,0:T(8,128)(2,1)} %copy-done.22) | copy-start | bytes 1204228
  211.3 16.2 %collective-permute-start.18 = (bf16[49,16,256]{2,1,0:T(8,128)(2,1)S(1)}, bf16[49,16,256]{2,1,0:T(8,128)(2,1)S(1)}, u32[]{:S(2)}, u32[]{:S(2)}) collective-permute-start(bf16[49,16,256]{2,1,0:T(8,128)(2,1)S(1)} %get-tuple-element.201), channel_id=1, source_target_pairs={{0,32},{32,64},{64,96},{96,0},{1,33},{33,65},{65,97},{97,1},{2,34}... | collective-permute-start | bytes 1204232 | tf_op jit(solution)/shard_map/ppermute | solution.py:478
  212.6 22.4 %collective-permute-start.19 = (bf16[49,16,256]{2,1,0:T(8,128)(2,1)S(1)}, bf16[49,16,256]{2,1,0:T(8,128)(2,1)S(1)}, u32[]{:S(2)}, u32[]{:S(2)}) collective-permute-start(bf16[49,16,256]{2,1,0:T(8,128)(2,1)S(1)} %get-tuple-element.202), channel_id=1, source_target_pairs={{0,64},{32,96},{64,0},{96,32},{1,65},{33,97},{65,1},{97,33},{2,66}... | collective-permute-start | bytes 1204232 | tf_op jit(solution)/shard_map/ppermute | solution.py:478
  215.0 20.0 %collective-permute-start.20 = (bf16[49,16,256]{2,1,0:T(8,128)(2,1)S(1)}, bf16[49,16,256]{2,1,0:T(8,128)(2,1)S(1)}, u32[]{:S(2)}, u32[]{:S(2)}) collective-permute-start(bf16[49,16,256]{2,1,0:T(8,128)(2,1)S(1)} %get-tuple-element.203), channel_id=1, source_target_pairs={{0,96},{32,0},{64,32},{96,64},{1,97},{33,1},{65,33},{97,65},{2,98}... | collective-permute-start | bytes 1204232 | tf_op jit(solution)/shard_map/ppermute | solution.py:478
  (14 other events, 128.2 us)
Sparse Core Ops, SparseCore 0:
  58.2 76.2 all-gather.1
